TPU v7x, 256 devices: a whole 4x4x8 slice. The times are simulated.
256 devices in a mesh: tile: 32 (over z_hi, x, y), day: 8 (over z_lo, core).
Axes of the slice: x: 4, y: 4, z: 8 (z_hi: 2, z_lo: 4; z = z_hi * 4 + z_lo), core: 2. Of those that a mesh axis runs over, the one named last changes fastest.
Arguments:
- spectra: bfloat16 [8192, 24, 6, 1024], P('tile', 'day'), may hold values from -6 to 6
- send_list: int32 [4096], P('tile'), may hold values from 0 to 255
- pair_first: int32 [32768], P('tile'), may hold values from 0 to 255
- pair_second: int32 [32768], P('tile'), may hold values from 0 to 383, as said below
Outputs:
- stacked_corr: float32 [32768, 1001], P(('tile', 'day'))
Inputs may be any that keep to these rules, and one draw needn't show every extreme that they name: `pair_second`: slots 0 to 255 of the table are the tile's own stations, the next 64 come from the tile below and the last 64 from the tile above; the first tile's pairs never use slots from below, the last tile's never those from above.
All inputs are finite; a program needn't handle non-finite values.
Results may differ from a plain program's by a relative error of at most 0.0003.
Values may be sent and summed in bfloat16 or wider, within the bound.
No kernel may reach another device: no remote copies, remote signals or barrier semaphores. Data moves between devices by JAX's collectives and lax.ppermute only.
A program may use at most 128 MiB of HBM per device.

v0:
```python
import math

import jax
import jax.numpy as jnp
from jax import lax
from jax.sharding import PartitionSpec as P

HALF_LAG = 500


def padded_2(cells, sides, width):
    for axis, dim in sides:
        count = lax.axis_size(axis)
        ends = count - 1
        head = lax.slice_in_dim(cells, 0, width, axis=dim)
        tail = lax.slice_in_dim(cells, cells.shape[dim] - width, cells.shape[dim], axis=dim)
        cells = jnp.concatenate(
            [
                lax.ppermute(tail, axis, [(i, (i + 1) % count) for i in range(ends)]),
                cells,
                lax.ppermute(head, axis, [((i + 1) % count, i) for i in range(ends)]),
            ],
            axis=dim,
        )
    return cells


def lag_table(freq_bins, half_lag):
    column = jnp.arange(freq_bins, dtype=jnp.int32)[:, None]
    shifts = jnp.arange(2 * half_lag + 1, dtype=jnp.int32)[None, :] - half_lag
    phases = column * shifts % (2 * freq_bins)
    angles = phases.astype(jnp.float32) * (math.pi / freq_bins)
    return jnp.concatenate([jnp.cos(angles), -jnp.sin(angles)], axis=0)


def cross_flat(first_rows, second_rows, freq_bins, groups):
    real_part = jnp.zeros((first_rows.shape[0], freq_bins), jnp.float32)
    imag_part = jnp.zeros((first_rows.shape[0], freq_bins), jnp.float32)
    for group in range(groups):
        offset = group * 2 * freq_bins
        first_real = first_rows[:, offset : offset + freq_bins].astype(jnp.float32)
        first_imag = first_rows[:, offset + freq_bins : offset + 2 * freq_bins].astype(jnp.float32)
        second_real = second_rows[:, offset : offset + freq_bins].astype(jnp.float32)
        second_imag = second_rows[:, offset + freq_bins : offset + 2 * freq_bins].astype(
            jnp.float32
        )
        real_part = real_part + (first_real * second_real + first_imag * second_imag)
        imag_part = imag_part + (first_imag * second_real - first_real * second_imag)
    return jnp.concatenate([real_part, imag_part], axis=-1)


def pair_spectra(own_flat, table_flat, first_ids, second_ids, freq_bins, groups):
    count = first_ids.shape[0]
    width = min(count, 128)
    first_blocks = first_ids.reshape(count // width, width)
    second_blocks = second_ids.reshape(count // width, width)

    def one_block(ids):
        return cross_flat(own_flat[ids[0]], table_flat[ids[1]], freq_bins, groups)

    result = lax.map(one_block, (first_blocks, second_blocks))
    return result.reshape(count, 2 * freq_bins)


def per_device(spectra, send_list, pair_first, pair_second):
    halo_width = send_list.shape[0] // 2
    freq_bins = spectra.shape[-1] // 2
    groups = spectra.shape[1] * spectra.shape[2]
    own_flat = spectra.reshape(spectra.shape[0], groups * 2 * freq_bins)
    border = own_flat[send_list]
    padded = padded_2(border, (("tile", 0),), halo_width)
    table_flat = jnp.concatenate(
        [own_flat, padded[:halo_width], padded[padded.shape[0] - halo_width :]], axis=0
    )
    cross = pair_spectra(own_flat, table_flat, pair_first, pair_second, freq_bins, groups)
    weights = lag_table(freq_bins, HALF_LAG)
    scale = 1.0 / math.sqrt(
        2 * freq_bins * spectra.shape[2] * spectra.shape[1] * lax.axis_size("day")
    )
    partial_lags = (
        jnp.dot(cross, weights, precision=lax.Precision.HIGHEST, preferred_element_type=jnp.float32)
        * scale
    )
    return lax.psum_scatter(partial_lags, "day", scatter_dimension=0, tiled=True)


def solution(mesh):
    placed = (P("tile", "day", None, None), P("tile"), P("tile"), P("tile"))
    return jax.shard_map(
        per_device, mesh=mesh, in_specs=placed, out_specs=P(("tile", "day"), None), check_vma=False
    )
```

profile of v0, /device:TPU:95, one launch (start us, length us, event | category | flops | bytes accessed | tf_op | source)
XLA Modules:
  0.0 622.9 jit_solution(2401144000646887677)
XLA Ops:
  6.5 12.7 %copy.6 = bf16[256,3,6,1024]{0,3,2,1:T(8,128)(2,1)} copy(bf16[256,3,6,1024]{3,0,2,1:T(8,128)(2,1)} %param.6) | data formatting | bytes 18874368 | tf_op args[0]
  19.3 12.7 %copy.10 = bf16[256,18432]{1,0:T(8,128)(2,1)} copy(bf16[256,18432]{0,1:T(8,128)(2,1)} %bitcast.31) | data formatting | bytes 18874368 | tf_op jit(solution)/shard_map/while | solution.py:61
  32.0 14.7 %gather_fusion.2 = bf16[128,18432]{1,0:T(8,128)(2,1)} fusion(bf16[256,18432]{1,0:T(8,128)(2,1)} %copy.10, s32[1024]{0:T(1024)S(1)} %pad_clamp_fusion.2), kind=kCustom, calls=%fused_computation.2 | custom fusion | bytes 9437696 | tf_op jit(solution)/shard_map/gather | solution.py:70
  46.7 4.9 fusion.90
  51.6 6.6 %collective-permute-start = (bf16[64,18432]{1,0:T(8,128)(2,1)}, bf16[64,18432]{1,0:T(8,128)(2,1)}, u32[]{:S(2)}, u32[]{:S(2)}) collective-permute-start(bf16[64,18432]{1,0:T(8,128)(2,1)} %get-tuple-element.58), channel_id=1, source_target_pairs={{0,8},{8,16},{16,24},{24,32},{32,40},{40,48},{48,56},{56,64},{64,7... | collective-permute-start | bytes 7077896 | tf_op jit(solution)/shard_map/ppermute | solution.py:19
  58.2 18.2 %collective-permute-start.1 = (bf16[64,18432]{1,0:T(8,128)(2,1)}, bf16[64,18432]{1,0:T(8,128)(2,1)S(1)}, u32[]{:S(2)}, u32[]{:S(2)}) collective-permute-start(bf16[64,18432]{1,0:T(8,128)(2,1)} %get-tuple-element.59), channel_id=1, source_target_pairs={{8,0},{16,8},{24,16},{32,24},{40,32},{48,40},{56,48},{64,56},{72,6... | collective-permute-start | bytes 7077896 | tf_op jit(solution)/shard_map/ppermute | solution.py:21
  76.4 9.3 %fusion.88 = (f32[512,1001]{1,0:T(8,128)}, f32[512,1001]{1,0:T(8,128)}) fusion(s32[1001]{0:T(1024)S(1)} %iota_add_fusion), kind=kLoop, calls=%fused_computation.173 | loop fusion | flops 7687680 | bytes 4104100 | tf_op jit(solution)/shard_map/cos | solution.py:33
  85.8 73.4 %collective-permute-done = bf16[64,18432]{1,0:T(8,128)(2,1)} collective-permute-done((bf16[64,18432]{1,0:T(8,128)(2,1)}, bf16[64,18432]{1,0:T(8,128)(2,1)}, u32[]{:S(2)}, u32[]{:S(2)}) %collective-permute-start) | collective-permute-done | bytes 2359328 | tf_op jit(solution)/shard_map/ppermute | solution.py:19
  159.1 5.7 copy.8
  164.8 6.4 %collective-permute-done.1 = bf16[64,18432]{1,0:T(8,128)(2,1)S(1)} collective-permute-done((bf16[64,18432]{1,0:T(8,128)(2,1)}, bf16[64,18432]{1,0:T(8,128)(2,1)S(1)}, u32[]{:S(2)}, u32[]{:S(2)}) %collective-permute-start.1) | collective-permute-done | bytes 2359328 | tf_op jit(solution)/shard_map/ppermute | solution.py:21
  171.2 4.1 copy.9
  175.4 16.4 %pad_maximum_fusion = bf16[384,18432]{0,1:T(8,128)(2,1)} fusion(bf16[64,18432]{0,1:T(8,128)(2,1)} %copy.9, bf16[64,18432]{0,1:T(8,128)(2,1)} %copy.8, bf16[256,18432]{0,1:T(8,128)(2,1)} %bitcast.32), kind=kLoop, calls=%fused_computation.157 | loop fusion | flops 42467328 | bytes 28311552 | tf_op jit(solution)/shard_map/concatenate | solution.py:72
  191.8 18.7 %copy.11 = bf16[384,18432]{1,0:T(8,128)(2,1)} copy(bf16[384,18432]{0,1:T(8,128)(2,1)} %pad_maximum_fusion) | data formatting | bytes 28311552 | tf_op jit(solution)/shard_map/while | solution.py:61
  210.4 336.9 %while.10 = (s32[]{:T(128)}, f32[8,128,1024]{2,1,0:T(8,128)}, s32[8,128]{1,0:T(8,128)}, bf16[256,18432]{1,0:T(8,128)(2,1)}, s32[8,128]{1,0:T(8,128)}, /*index=5*/bf16[384,18432]{1,0:T(8,128)(2,1)}, s32[]{:T(128)}) while((s32[]{:T(128)}, f32[8,128,1024]{2,1,0:T(8,128)}, s32[8,128]{1,0:T(8,128)}, bf16[256,18432]{1,0:T(8,128)(2,1)}, ...), condition=%wide.region_1.2_spmd, body=%wide.region_0.1_spmd.sunk | while | flops 18877184 | bytes 77083272 | solution.py:61
  211.3 16.6 %gather_fusion = bf16[128,18432]{1,0:T(8,128)(2,1)} fusion(bf16[384,18432]{1,0:T(8,128)(2,1)} %get-tuple-element.122, s32[1024]{0:T(1024)S(1)} %pad_clamp_fusion.5), kind=kCustom, calls=%fused_computation.1.clone.1 | custom fusion | bytes 9437696 | tf_op jit(solution)/shard_map/while/body/eval_jaxpr/gather | solution.py:59
  227.9 14.7 %gather_fusion.1 = bf16[128,18432]{1,0:T(8,128)(2,1)} fusion(bf16[256,18432]{1,0:T(8,128)(2,1)} %get-tuple-element.120, s32[1024]{0:T(1024)S(1)} %pad_clamp_fusion.6), kind=kCustom, calls=%fused_computation.clone.1 | custom fusion | bytes 9437696 | tf_op jit(solution)/shard_map/while/body/eval_jaxpr/gather | solution.py:59
  242.6 5.0 fusion.98
  249.3 2.5 fusion.97
  253.4 16.6 %gather_fusion = bf16[128,18432]{1,0:T(8,128)(2,1)} fusion(bf16[384,18432]{1,0:T(8,128)(2,1)} %get-tuple-element.122, s32[1024]{0:T(1024)S(1)} %pad_clamp_fusion.5), kind=kCustom, calls=%fused_computation.1.clone.1 | custom fusion | bytes 9437696 | tf_op jit(solution)/shard_map/while/body/eval_jaxpr/gather | solution.py:59
  270.0 14.7 %gather_fusion.1 = bf16[128,18432]{1,0:T(8,128)(2,1)} fusion(bf16[256,18432]{1,0:T(8,128)(2,1)} %get-tuple-element.120, s32[1024]{0:T(1024)S(1)} %pad_clamp_fusion.6), kind=kCustom, calls=%fused_computation.clone.1 | custom fusion | bytes 9437696 | tf_op jit(solution)/shard_map/while/body/eval_jaxpr/gather | solution.py:59
  284.7 5.0 fusion.98
  291.4 2.5 fusion.97
  295.5 16.6 %gather_fusion = bf16[128,18432]{1,0:T(8,128)(2,1)} fusion(bf16[384,18432]{1,0:T(8,128)(2,1)} %get-tuple-element.122, s32[1024]{0:T(1024)S(1)} %pad_clamp_fusion.5), kind=kCustom, calls=%fused_computation.1.clone.1 | custom fusion | bytes 9437696 | tf_op jit(solution)/shard_map/while/body/eval_jaxpr/gather | solution.py:59
  312.1 14.7 %gather_fusion.1 = bf16[128,18432]{1,0:T(8,128)(2,1)} fusion(bf16[256,18432]{1,0:T(8,128)(2,1)} %get-tuple-element.120, s32[1024]{0:T(1024)S(1)} %pad_clamp_fusion.6), kind=kCustom, calls=%fused_computation.clone.1 | custom fusion | bytes 9437696 | tf_op jit(solution)/shard_map/while/body/eval_jaxpr/gather | solution.py:59
  326.8 5.0 fusion.98
  333.5 2.5 fusion.97
  337.6 16.6 %gather_fusion = bf16[128,18432]{1,0:T(8,128)(2,1)} fusion(bf16[384,18432]{1,0:T(8,128)(2,1)} %get-tuple-element.122, s32[1024]{0:T(1024)S(1)} %pad_clamp_fusion.5), kind=kCustom, calls=%fused_computation.1.clone.1 | custom fusion | bytes 9437696 | tf_op jit(solution)/shard_map/while/body/eval_jaxpr/gather | solution.py:59
  354.2 14.7 %gather_fusion.1 = bf16[128,18432]{1,0:T(8,128)(2,1)} fusion(bf16[256,18432]{1,0:T(8,128)(2,1)} %get-tuple-element.120, s32[1024]{0:T(1024)S(1)} %pad_clamp_fusion.6), kind=kCustom, calls=%fused_computation.clone.1 | custom fusion | bytes 9437696 | tf_op jit(solution)/shard_map/while/body/eval_jaxpr/gather | solution.py:59
  368.9 5.0 fusion.98
  375.6 2.5 fusion.97
  379.7 16.6 %gather_fusion = bf16[128,18432]{1,0:T(8,128)(2,1)} fusion(bf16[384,18432]{1,0:T(8,128)(2,1)} %get-tuple-element.122, s32[1024]{0:T(1024)S(1)} %pad_clamp_fusion.5), kind=kCustom, calls=%fused_computation.1.clone.1 | custom fusion | bytes 9437696 | tf_op jit(solution)/shard_map/while/body/eval_jaxpr/gather | solution.py:59
  396.3 14.7 %gather_fusion.1 = bf16[128,18432]{1,0:T(8,128)(2,1)} fusion(bf16[256,18432]{1,0:T(8,128)(2,1)} %get-tuple-element.120, s32[1024]{0:T(1024)S(1)} %pad_clamp_fusion.6), kind=kCustom, calls=%fused_computation.clone.1 | custom fusion | bytes 9437696 | tf_op jit(solution)/shard_map/while/body/eval_jaxpr/gather | solution.py:59
  411.0 5.0 fusion.98
  417.7 2.5 fusion.97
  421.8 16.6 %gather_fusion = bf16[128,18432]{1,0:T(8,128)(2,1)} fusion(bf16[384,18432]{1,0:T(8,128)(2,1)} %get-tuple-element.122, s32[1024]{0:T(1024)S(1)} %pad_clamp_fusion.5), kind=kCustom, calls=%fused_computation.1.clone.1 | custom fusion | bytes 9437696 | tf_op jit(solution)/shard_map/while/body/eval_jaxpr/gather | solution.py:59
  438.4 14.7 %gather_fusion.1 = bf16[128,18432]{1,0:T(8,128)(2,1)} fusion(bf16[256,18432]{1,0:T(8,128)(2,1)} %get-tuple-element.120, s32[1024]{0:T(1024)S(1)} %pad_clamp_fusion.6), kind=kCustom, calls=%fused_computation.clone.1 | custom fusion | bytes 9437696 | tf_op jit(solution)/shard_map/while/body/eval_jaxpr/gather | solution.py:59
  453.1 5.0 fusion.98
  459.8 2.5 fusion.97
  463.9 16.6 %gather_fusion = bf16[128,18432]{1,0:T(8,128)(2,1)} fusion(bf16[384,18432]{1,0:T(8,128)(2,1)} %get-tuple-element.122, s32[1024]{0:T(1024)S(1)} %pad_clamp_fusion.5), kind=kCustom, calls=%fused_computation.1.clone.1 | custom fusion | bytes 9437696 | tf_op jit(solution)/shard_map/while/body/eval_jaxpr/gather | solution.py:59
  480.5 14.7 %gather_fusion.1 = bf16[128,18432]{1,0:T(8,128)(2,1)} fusion(bf16[256,18432]{1,0:T(8,128)(2,1)} %get-tuple-element.120, s32[1024]{0:T(1024)S(1)} %pad_clamp_fusion.6), kind=kCustom, calls=%fused_computation.clone.1 | custom fusion | bytes 9437696 | tf_op jit(solution)/shard_map/while/body/eval_jaxpr/gather | solution.py:59
  495.2 5.0 fusion.98
  501.9 2.5 fusion.97
  506.0 16.6 %gather_fusion = bf16[128,18432]{1,0:T(8,128)(2,1)} fusion(bf16[384,18432]{1,0:T(8,128)(2,1)} %get-tuple-element.122, s32[1024]{0:T(1024)S(1)} %pad_clamp_fusion.5), kind=kCustom, calls=%fused_computation.1.clone.1 | custom fusion | bytes 9437696 | tf_op jit(solution)/shard_map/while/body/eval_jaxpr/gather | solution.py:59
  522.5 14.7 %gather_fusion.1 = bf16[128,18432]{1,0:T(8,128)(2,1)} fusion(bf16[256,18432]{1,0:T(8,128)(2,1)} %get-tuple-element.120, s32[1024]{0:T(1024)S(1)} %pad_clamp_fusion.6), kind=kCustom, calls=%fused_computation.clone.1 | custom fusion | bytes 9437696 | tf_op jit(solution)/shard_map/while/body/eval_jaxpr/gather | solution.py:59
  537.2 5.0 fusion.98
  543.9 2.5 fusion.97
  547.3 17.0 %fusion.79 = f32[1024,1001]{0,1:T(8,128)} fusion(f32[1024,1024]{1,0:T(8,128)} %bitcast.8, f32[512,1001]{1,0:T(8,128)} %get-tuple-element.61, f32[512,1001]{1,0:T(8,128)S(1)} %copy-done.2), kind=kOutput, calls=%fused_computation.165 | convolution fusion | flops 12597544960 | bytes 12394496 | tf_op jit(solution)/shard_map/dot_general | solution.py:81
  564.4 51.4 %reduce-scatter.2.cloned.1.call-done = f32[128,1001]{0,1:T(8,128)} async-done(((f32[1024,1001]{0,1:T(8,128)}), f32[128,1001]{0,1:T(8,128)}) %reduce-scatter.2.cloned.1.call-update) | async-done | bytes 512528 | tf_op jit(solution)/shard_map/reduce_scatter | solution.py:84
  (74 shorter events, 26.1 us)
Async XLA Ops:
  6.5 609.2 %reduce-scatter.2.cloned.1.call-start = ((), (), s32[]{:S(2)}) async-start(), calls=%async_computation.1 | async-start | bytes 4644864 | tf_op jit(solution)/shard_map/reduce_scatter | solution.py:84
  19.3 12.7 %copy-start.3 = (s32[128]{0:T(128)S(1)}, s32[128]{0:T(128)}, u32[]{:S(2)}) copy-start(s32[128]{0:T(128)} %param.7) | copy-start | bytes 1540
  51.6 107.5 %collective-permute-start = (bf16[64,18432]{1,0:T(8,128)(2,1)}, bf16[64,18432]{1,0:T(8,128)(2,1)}, u32[]{:S(2)}, u32[]{:S(2)}) collective-permute-start(bf16[64,18432]{1,0:T(8,128)(2,1)} %get-tuple-element.58), channel_id=1, source_target_pairs={{0,8},{8,16},{16,24},{24,32},{32,40},{40,48},{48,56},{56,64},{64,7... | collective-permute-start | bytes 7077896 | tf_op jit(solution)/shard_map/ppermute | solution.py:19
  58.2 113.0 %collective-permute-start.1 = (bf16[64,18432]{1,0:T(8,128)(2,1)}, bf16[64,18432]{1,0:T(8,128)(2,1)S(1)}, u32[]{:S(2)}, u32[]{:S(2)}) collective-permute-start(bf16[64,18432]{1,0:T(8,128)(2,1)} %get-tuple-element.59), channel_id=1, source_target_pairs={{8,0},{16,8},{24,16},{32,24},{40,32},{48,40},{56,48},{64,56},{72,6... | collective-permute-start | bytes 7077896 | tf_op jit(solution)/shard_map/ppermute | solution.py:21
  210.4 336.9 %copy-start.2 = (f32[512,1001]{1,0:T(8,128)S(1)}, f32[512,1001]{1,0:T(8,128)}, u32[]{:S(2)}) copy-start(f32[512,1001]{1,0:T(8,128)} %get-tuple-element.60) | copy-start | bytes 6150148
  242.6 5.2 copy-start
  242.6 6.7 %copy-start.1 = (bf16[128,18432]{1,0:T(8,128)(2,1)S(1)}, bf16[128,18432]{1,0:T(8,128)(2,1)}, u32[]{:S(2)}) copy-start(bf16[128,18432]{1,0:T(8,128)(2,1)} %gather_fusion.1) | copy-start | bytes 14155780 | tf_op jit(solution)/shard_map/while
  284.7 5.2 copy-start
  284.7 6.7 %copy-start.1 = (bf16[128,18432]{1,0:T(8,128)(2,1)S(1)}, bf16[128,18432]{1,0:T(8,128)(2,1)}, u32[]{:S(2)}) copy-start(bf16[128,18432]{1,0:T(8,128)(2,1)} %gather_fusion.1) | copy-start | bytes 14155780 | tf_op jit(solution)/shard_map/while
  326.8 5.2 copy-start
  326.8 6.7 %copy-start.1 = (bf16[128,18432]{1,0:T(8,128)(2,1)S(1)}, bf16[128,18432]{1,0:T(8,128)(2,1)}, u32[]{:S(2)}) copy-start(bf16[128,18432]{1,0:T(8,128)(2,1)} %gather_fusion.1) | copy-start | bytes 14155780 | tf_op jit(solution)/shard_map/while
  368.9 5.2 copy-start
  368.9 6.7 %copy-start.1 = (bf16[128,18432]{1,0:T(8,128)(2,1)S(1)}, bf16[128,18432]{1,0:T(8,128)(2,1)}, u32[]{:S(2)}) copy-start(bf16[128,18432]{1,0:T(8,128)(2,1)} %gather_fusion.1) | copy-start | bytes 14155780 | tf_op jit(solution)/shard_map/while
  411.0 5.2 copy-start
  411.0 6.7 %copy-start.1 = (bf16[128,18432]{1,0:T(8,128)(2,1)S(1)}, bf16[128,18432]{1,0:T(8,128)(2,1)}, u32[]{:S(2)}) copy-start(bf16[128,18432]{1,0:T(8,128)(2,1)} %gather_fusion.1) | copy-start | bytes 14155780 | tf_op jit(solution)/shard_map/while
  453.1 5.2 copy-start
  453.1 6.7 %copy-start.1 = (bf16[128,18432]{1,0:T(8,128)(2,1)S(1)}, bf16[128,18432]{1,0:T(8,128)(2,1)}, u32[]{:S(2)}) copy-start(bf16[128,18432]{1,0:T(8,128)(2,1)} %gather_fusion.1) | copy-start | bytes 14155780 | tf_op jit(solution)/shard_map/while
  495.2 5.2 copy-start
  495.2 6.7 %copy-start.1 = (bf16[128,18432]{1,0:T(8,128)(2,1)S(1)}, bf16[128,18432]{1,0:T(8,128)(2,1)}, u32[]{:S(2)}) copy-start(bf16[128,18432]{1,0:T(8,128)(2,1)} %gather_fusion.1) | copy-start | bytes 14155780 | tf_op jit(solution)/shard_map/while
  537.2 5.2 copy-start
  537.2 6.7 %copy-start.1 = (bf16[128,18432]{1,0:T(8,128)(2,1)S(1)}, bf16[128,18432]{1,0:T(8,128)(2,1)}, u32[]{:S(2)}) copy-start(bf16[128,18432]{1,0:T(8,128)(2,1)} %gather_fusion.1) | copy-start | bytes 14155780 | tf_op jit(solution)/shard_map/while
Sparse Core Ops, SparseCore 0:
  564.5 51.1 reduce-scatter.1
where the time goes:
time: 635 us; the launch traced here: 623 us
  local copies, waits for them, and re-layouts  337 us (53%)
  waiting for transfers between devices  131 us (21%)
  other arithmetic  98.8 us (16%)
  starting transfers between devices  24.8 us (4%)
  matrix products  17 us (3%)
  between operations  13.8 us (2%)
    gather x16, local copies, waits for them, and re-layouts, one_block(): return cross_flat(own_flat[ids[0]], table_flat[ids[1]], freq_bins, groups)  250 us
    ppermute x1, waiting for transfers between devices, padded_2(): lax.ppermute(tail, axis, [(i, (i + 1) % count) for i in range(ends)])  73.4 us
    reduce_scatter x1, waiting for transfers between devices, per_device(): lax.psum_scatter(partial_lags, 'day', scatter_dimension=0, tiled=True)  51.4 us
    add x8, other arithmetic, cross_flat(): real_part + (first_real * second_real + first_imag * second_imag)  40 us
    while x2, local copies, waits for them, and re-layouts, pair_spectra(): result = lax.map(one_block, (first_blocks, second_blocks))  31.3 us
    add x8, other arithmetic, cross_flat(): imag_part + (first_imag * second_real - first_real * second_imag)  20.4 us
    ppermute x1, starting transfers between devices, padded_2(): lax.ppermute(head, axis, [((i + 1) % count, i) for i in range(ends)])  18.2 us
    dot_general x1, matrix products, per_device(): jnp.dot(cross, weights, precision=lax.Precision.HIGHEST, preferred_elemen...  17 us
  transfers between devices with their start and end apart: 3, of which 3 were waited for; matrix products, arithmetic and copies ran while one was open for 2% of the time, Pallas kernels for 0%

commit v1 on v0

v1 whole, which is shorter than its diff:
```python
import functools

import jax
import jax.numpy as jnp
import numpy as np
from jax import lax
from jax.experimental import pallas as pl
from jax.experimental.pallas import tpu as pltpu
from jax.sharding import PartitionSpec as P

HALF_LAG = 500
LANES = 128
CHUNKS = ((0, 1), (2, 3))
PAIR_BLOCK = 256
SEG_STEP = 6
VMEM = 60 << 20
SCALE_ROWS = 16
TOP = 32000.0


def one_hot(ids, width, base):
    slots = lax.broadcasted_iota(jnp.int32, (ids.shape[0], width), 1) + base
    return (ids == slots).astype(jnp.float32).astype(jnp.bfloat16)


def anywhere():
    return pl.BlockSpec(memory_space=pl.ANY)


def scalars():
    return pl.BlockSpec(memory_space=pltpu.SMEM)


def params():
    return pltpu.CompilerParams(vmem_limit_bytes=VMEM)


def border_kernel(flag_ref, send_ref, real_ref, imag_ref, below_ref, above_ref, next_ref, pick_ref):
    next_ref[0] = flag_ref[0]

    @pl.when((pl.program_id(0) == 0) & (pl.program_id(1) == 0))
    def _():
        pick_ref[...] = one_hot(send_ref[...], pick_ref.shape[1], 0)

    half = below_ref.shape[1]
    step = real_ref.shape[0]
    for seg in range(step):
        rows = jnp.concatenate([real_ref[seg], imag_ref[seg]], axis=1)
        lent = jnp.dot(pick_ref[...], rows, preferred_element_type=jnp.float32)
        lent = lent.astype(jnp.bfloat16)
        below_ref[seg] = lent[:half]
        above_ref[seg] = lent[half:]


def lent_rows(flags, spectra, send_list, chunk):
    groups, stations, width = spectra.shape
    count = send_list.shape[0]
    half = count // 2
    first, blocks = chunk[0], len(chunk)
    offset = width // 2 // LANES
    step = 9
    lanes = 2 * LANES * blocks
    out = jax.ShapeDtypeStruct((groups, half, lanes), jnp.bfloat16)
    out_spec = pl.BlockSpec((step, half, 2 * LANES), lambda j, g: (g, 0, j))
    return pl.pallas_call(
        border_kernel,
        grid=(blocks, groups // step),
        in_specs=[
            scalars(),
            pl.BlockSpec((count, 1), lambda j, g: (0, 0)),
            pl.BlockSpec((step, stations, LANES), lambda j, g: (g, 0, first + j)),
            pl.BlockSpec((step, stations, LANES), lambda j, g: (g, 0, first + j + offset)),
        ],
        out_specs=[out_spec, out_spec, scalars()],
        out_shape=[out, out, jax.ShapeDtypeStruct((1,), jnp.int32)],
        scratch_shapes=[pltpu.VMEM((count, stations), jnp.bfloat16)],
        compiler_params=params(),
        cost_estimate=pl.CostEstimate(
            flops=2 * count * stations * groups * lanes,
            bytes_accessed=groups * (stations + count) * lanes * 2,
            transcendentals=0,
        ),
    )(flags, send_list.reshape(count, 1), spectra, spectra)


def cross_kernel(
    flag_ref, first_ref, second_ref, real_ref, imag_ref, below_ref, above_ref, relay_ref, token_ref,
    send_ref, keep_ref, own_ref, halo_ref, border_ref,
):
    stations = real_ref.shape[1]
    lent = below_ref.shape[1]
    blocks = own_ref.shape[0]
    size = halo_ref.shape[1]
    groups = real_ref.shape[0]
    turn = pl.program_id(1)

    @pl.when((pl.program_id(0) == 0) & (turn == 0))
    def _():
        for block in range(blocks):
            rows = slice(block * size, (block + 1) * size)
            own_ref[block, :size] = one_hot(first_ref[rows], stations, 0)
            own_ref[block, size:] = one_hot(second_ref[rows], stations, 0)
            halo_ref[block] = one_hot(second_ref[rows], 2 * lent, stations)

    @pl.when(turn == 0)
    def _():
        send_ref[...] = jnp.zeros_like(send_ref)
        keep_ref[...] = jnp.zeros_like(keep_ref)

    border_ref[:, :lent] = below_ref[...]
    border_ref[:, lent:] = above_ref[...]

    @pl.when(flag_ref[0] == 1)
    def _():
        border_ref[:, :lent] = relay_ref[...]

    @pl.when(flag_ref[0] == 2)
    def _():
        border_ref[:, lent:] = relay_ref[...]

    for block in range(blocks):
        out_ref = (send_ref, keep_ref)[block // (blocks // 2)]
        start = block % (blocks // 2) * size
        rows = slice(start, start + size)
        real = out_ref[rows, :LANES]
        imag = out_ref[rows, LANES:]
        for seg in range(groups):
            table = jnp.concatenate([real_ref[seg], imag_ref[seg]], axis=1)
            both = jnp.dot(own_ref[block], table, preferred_element_type=jnp.float32)
            a = both[:size]
            b = both[size:] + jnp.dot(halo_ref[block], border_ref[seg], preferred_element_type=jnp.float32)
            ar, ai, br, bi = a[:, :LANES], a[:, LANES:], b[:, :LANES], b[:, LANES:]
            real = real + (ar * br + ai * bi)
            imag = imag + (ai * br - ar * bi)
        out_ref[rows, :LANES] = real
        out_ref[rows, LANES:] = imag


def pair_cross(flags, first_ids, second_ids, spectra, halo, chunk, token):
    below, above, relay = halo
    groups, stations, width = spectra.shape
    pairs = first_ids.shape[0]
    lent = below.shape[1]
    offset = width // 2 // LANES
    blocks = pairs // PAIR_BLOCK
    first, parts = chunk[0], len(chunk)
    ids_spec = pl.BlockSpec((pairs, 1), lambda j, g: (0, 0))
    halo_spec = pl.BlockSpec((SEG_STEP, lent, 2 * LANES), lambda j, g: (g, 0, j))

    out = jax.ShapeDtypeStruct((pairs // 2, 2 * LANES * parts), jnp.float32)
    return pl.pallas_call(
        cross_kernel,
        grid=(parts, groups // SEG_STEP),
        in_specs=[
            scalars(),
            ids_spec,
            ids_spec,
            pl.BlockSpec((SEG_STEP, stations, LANES), lambda j, g: (g, 0, first + j)),
            pl.BlockSpec((SEG_STEP, stations, LANES), lambda j, g: (g, 0, first + j + offset)),
            halo_spec,
            halo_spec,
            halo_spec,
            anywhere(),
        ],
        out_specs=[pl.BlockSpec((pairs // 2, 2 * LANES), lambda j, g: (0, j))] * 2,
        out_shape=[out, out],
        scratch_shapes=[
            pltpu.VMEM((blocks, 2 * PAIR_BLOCK, stations), jnp.bfloat16),
            pltpu.VMEM((blocks, PAIR_BLOCK, 2 * lent), jnp.bfloat16),
            pltpu.VMEM((SEG_STEP, 2 * lent, 2 * LANES), jnp.bfloat16),
        ],
        compiler_params=params(),
        cost_estimate=pl.CostEstimate(
            flops=2 * pairs * (2 * stations + 2 * lent) * groups * 2 * LANES * parts,
            bytes_accessed=groups * (stations + 2 * lent) * 2 * LANES * 2 * parts,
            transcendentals=0,
        ),
    )(flags, first_ids, second_ids, spectra, spectra, below, above, relay, token)


def pack_kernel(keep_ref, other_ref, token_ref, own_ref, *out_refs):
    kept = own_ref.shape[0]
    own_ref[...] = keep_ref[:kept] + other_ref[:kept]
    for k, out_ref in enumerate(out_refs, 1):
        rows = slice(k * kept, (k + 1) * kept)
        total = keep_ref[rows] + other_ref[rows]
        peak = jnp.max(jnp.abs(total), axis=0, keepdims=True)
        power = jnp.ceil(jnp.log2(jnp.maximum(peak, 1e-36) * 1.0001))
        scaled = jnp.round(total * jnp.exp2(-power) * TOP)
        out_ref[:kept] = scaled.astype(jnp.int32).astype(jnp.int16)
        powers = jnp.broadcast_to(power, (SCALE_ROWS, power.shape[1]))
        out_ref[kept:] = powers.astype(jnp.int32).astype(jnp.int16)


def pack(keep, other, token, parts):
    rows, lanes = keep.shape
    kept = rows // parts
    coded = jax.ShapeDtypeStruct((kept + SCALE_ROWS, lanes), jnp.int16)
    whole = pl.BlockSpec(memory_space=pltpu.VMEM)
    return pl.pallas_call(
        pack_kernel,
        in_specs=[whole, whole, anywhere()],
        out_specs=[whole] * parts,
        out_shape=[jax.ShapeDtypeStruct((kept, lanes), jnp.float32)] + [coded] * (parts - 1),
        compiler_params=params(),
    )(keep, other, token)


def unpack(ref, kept):
    power = ref[kept:].astype(jnp.int32).astype(jnp.float32)[:1]
    return ref[:kept].astype(jnp.int32).astype(jnp.float32) * (1.0 / TOP) * jnp.exp2(power)


def lag_kernel(parts, has_base, coarse_ref, fine_ref, *refs):
    out_ref = refs[-1]
    kept = refs[0].shape[0]
    blocks = []
    for place in range(0, len(refs) - 1 - has_base, parts):
        total = refs[place][...]
        for ref in refs[place + 1 : place + parts]:
            total = total + unpack(ref, kept)
        blocks.append(total)
    cross = jnp.concatenate(blocks, axis=1)
    high = cross.astype(jnp.bfloat16)
    low = (cross - high.astype(jnp.float32)).astype(jnp.bfloat16)
    dims = (((1,), (1,)), ((), ()))
    dot = functools.partial(lax.dot_general, dimension_numbers=dims, preferred_element_type=jnp.float32)
    lags = (dot(fine_ref[...], high) + dot(coarse_ref[...], low)) + dot(coarse_ref[...], high)
    if has_base:
        lags = lags + refs[-2][...]
    out_ref[...] = lags


def lag_sums(tables, blocks, base=None):
    parts = len(blocks[0])
    operands = [part for block in blocks for part in block] + ([] if base is None else [base])
    return pl.pallas_call(
        functools.partial(lag_kernel, parts, int(base is not None)),
        out_shape=jax.ShapeDtypeStruct((2 * HALF_LAG + 1, blocks[0][0].shape[0]), jnp.float32),
        compiler_params=params(),
    )(*tables, *operands)


def lag_tables(freq_bins, blocks, scale):
    lags = np.arange(2 * HALF_LAG + 1)[:, None] - HALF_LAG
    columns = []
    for block in blocks:
        bins = np.arange(block * LANES, (block + 1) * LANES)[None, :]
        angles = (bins * lags % (2 * freq_bins)) * (np.pi / freq_bins)
        columns += [np.cos(angles), -np.sin(angles)]
    table = (np.concatenate(columns, axis=1) * scale).astype(np.float32)
    coarse = table.astype(jnp.bfloat16)
    fine = (table - coarse.astype(np.float32)).astype(jnp.bfloat16)
    return jnp.asarray(coarse), jnp.asarray(fine)


def per_device(spectra, send_list, pair_first, pair_second):
    stations, days, segs, width = spectra.shape
    members = lax.axis_size("day")
    tiles = lax.axis_size("tile")
    me = lax.axis_index("day")
    tile = lax.axis_index("tile")
    groups = days * segs
    pairs = pair_first.shape[0]
    kept = pairs // members
    flat = jnp.transpose(spectra, (1, 2, 0, 3)).reshape(groups, stations, width)

    middle, last = tiles // 2, tiles - 1

    def shift(ahead):
        source, target, end = (middle - 1, middle, 0) if ahead else (middle, middle - 1, last)
        pairs = []
        for d in range(members):
            straight = (d >= members // 2) == ahead
            pairs.append((source * members + d, (target if straight else end) * members + d))
            for t in range(tiles - 1):
                if t + 1 != middle:
                    low, high = t * members + d, (t + 1) * members + d
                    pairs.append((low, high) if ahead else (high, low))
        return pairs

    upward, downward = shift(True), shift(False)
    onward = [(d, middle * members + d) for d in range(members // 2)]
    onward += [(last * members + d, (middle - 1) * members + d) for d in range(members // 2, members)]
    both = ("tile", "day")
    side = jnp.where((tile == middle) & (me < members // 2), 1, 0)
    side = jnp.where((tile == middle - 1) & (me >= members // 2), 2, side)
    side = jnp.where(tile == last, 3, side)
    flags = side.astype(jnp.int32).reshape(1)

    def swap(k):
        return [(i, i ^ k) for i in range(members)]

    sent = []
    for chunk in CHUNKS:
        to_below, to_above, flags = lent_rows(flags, flat, send_list, chunk)
        sent.append((lax.ppermute(to_above, both, upward), lax.ppermute(to_below, both, downward)))

    half = members // 2
    order = jnp.stack([me ^ (2 * k + 1) for k in range(half)] + [me ^ (2 * k) for k in range(half)])
    first_ids = pair_first.reshape(members, kept)[order].reshape(pairs, 1)
    second_ids = pair_second.reshape(members, kept)[order].reshape(pairs, 1)

    token = flags
    packed = []
    for chunk, (below, above) in zip(CHUNKS, sent):
        relay = lax.ppermute(jnp.where(flags[0] == 3, above, below), both, onward)
        halo = (below, above, relay)
        send, keep = pair_cross(flags, first_ids, second_ids, flat, halo, chunk, token)
        other = lax.ppermute(send, "day", swap(1))
        pieces = pack(keep, other, keep, half)
        packed.append(
            [pieces[0]]
            + [lax.ppermute(piece, "day", swap(2 * k)) for k, piece in enumerate(pieces) if k]
        )
        token = pieces[0]

    scale = 1.0 / np.sqrt(width * segs * days * members)
    early = [block for chunk in CHUNKS[:-1] for block in chunk]
    lags = lag_sums(lag_tables(width // 2, early, scale), packed[:-1])
    lags = lag_sums(lag_tables(width // 2, CHUNKS[-1], scale), packed[-1:], lags)
    return lags.T


def solution(mesh):
    placed = (P("tile", "day", None, None), P("tile"), P("tile"), P("tile"))
    return jax.shard_map(
        per_device, mesh=mesh, in_specs=placed, out_specs=P(("tile", "day"), None), check_vma=False
    )
```

time: 635 us -> 160 us (0.25); the launches traced: 623 us -> 159 us
  local copies, waits for them, and re-layouts: 337 us -> 8.9 us
  other arithmetic: 98.8 us -> 1.4 us
  waiting for transfers between devices: 131 us -> 53.8 us
  Pallas kernels: 0 us -> 64.9 us
  matrix products: 17 us -> 0 us
  between operations: 13.8 us -> 0.76 us
    gather x17 -> x2, local copies, waits for them, and re-layouts: 265 us -> 1.11 us  [the longest x1 0.56 us: per_device(): second_ids = pair_second.reshape(members, kept)[order].reshape(pairs, 1)]
    pallas_call x0 -> x8, Pallas kernels: none -> 64.9 us  [the longest x2 41.8 us: pair_cross(): pl.pallas_call(cross_kernel, grid=(parts, groups // SEG_STEP), in_specs=[...]
    add x16 -> x0, other arithmetic: 60.4 us -> none  [the longest x8 40 us: cross_flat(): real_part + (first_real * second_real + first_imag * second_imag)]
    reduce_scatter x1 -> x0, waiting for transfers between devices: 51.4 us -> none  [per_device(): lax.psum_scatter(partial_lags, 'day', scatter_dimension=0, tiled=True)]
    while x34 -> x0, local copies, waits for them, and re-layouts: 44.8 us -> none  [the longest x2 31.3 us: pair_spectra(): result = lax.map(one_block, (first_blocks, second_blocks))]
    ppermute x2 -> x14, waiting for transfers between devices: 79.7 us -> 53.8 us  [the longest x2 27.1 us: per_device(): lax.ppermute(to_above, both, upward)]
    dot_general x1 -> x0, matrix products: 17 us -> none  [per_device(): jnp.dot(cross, weights, precision=lax.Precision.HIGHEST, preferred_elemen...]
    concatenate x1 -> x0, other arithmetic: 16.4 us -> none  [per_device(): jnp.concatenate([own_flat, padded[:halo_width], padded[padded.shape[0] -...]
  transfers between devices with their start and end apart: 3 -> 14, of which waited for: 3 -> 8; matrix products, arithmetic and copies ran while one was open for 2% -> 3% of each run, Pallas kernels for 0% -> 22%
where the time goes in v1:
time: 160 us; the launch traced here: 159 us
  Pallas kernels  64.9 us (41%)
  waiting for transfers between devices  53.8 us (34%)
  starting transfers between devices  29.4 us (18%)
  local copies, waits for them, and re-layouts  8.9 us (6%)
    pallas_call x2, Pallas kernels, pair_cross(): pl.pallas_call(cross_kernel, grid=(parts, groups // SEG_STEP), in_specs=[...  41.8 us
    ppermute x2, waiting for transfers between devices, per_device(): lax.ppermute(to_above, both, upward)  27.1 us
    ppermute x6, waiting for transfers between devices, per_device(): lax.ppermute(piece, 'day', swap(2 * k))  15.4 us
    ppermute x2, starting transfers between devices, per_device(): lax.ppermute(to_above, both, upward)  12.4 us
    pallas_call x2, Pallas kernels, lent_rows(): pl.pallas_call(border_kernel, grid=(blocks, groups // step), in_specs=[sc...  10.8 us
    pallas_call x2, Pallas kernels, lag_sums(): pl.pallas_call(functools.partial(lag_kernel, parts, int(base is not None)...  7.32 us
    ppermute x2, waiting for transfers between devices, per_device(): relay = lax.ppermute(jnp.where(flags[0] == 3, above, below), both, onward)  6.09 us
    ppermute x6, starting transfers between devices, per_device(): lax.ppermute(piece, 'day', swap(2 * k))  5.46 us
  transfers between devices with their start and end apart: 14, of which 8 were waited for; matrix products, arithmetic and copies ran while one was open for 3% of the time, Pallas kernels for 22%

profile of v1, /device:TPU:95, one launch (start us, length us, event | category | flops | bytes accessed | tf_op | source)
XLA Modules:
  0.0 159.2 jit_solution(6420650467131725527)
XLA Ops:
  0.0 1.4 copy.11.send_ref
  1.4 5.0 %shard_map.82 = (bf16[18,64,512]{2,1,0:T(8,128)(2,1)}, bf16[18,64,512]{2,1,0:T(8,128)(2,1)}, s32[1]{0:T(128)}) custom-call(s32[1]{0:T(128)} %bitcast.flag_ref, s32[128,1]{1,0:T(8,128)} %copy.11.send_ref, bf16[18,256,1024]{2,1,0:T(8,128)(2,1)} %bitcast.22, bf16[18,256,1024]{2,1,0:T(8,128)(2,1)} %bitcast.23), custom_call_target="tpu_custom_call" | custom-call | flops 603979776 | bytes 7077888 | tf_op jit(solution)/shard_map/pallas_call | solution.py:65
  6.4 6.6 %collective-permute-start.3 = (bf16[18,64,512]{2,1,0:T(8,128)(2,1)}, bf16[18,64,512]{2,1,0:T(8,128)(2,1)S(1)}, u32[]{:S(2)}, u32[]{:S(2)}) collective-permute-start(bf16[18,64,512]{2,1,0:T(8,128)(2,1)} %get-tuple-element.27), channel_id=1, source_target_pairs={{120,0},{0,8},{8,16},{16,24},{24,32},{32,40},{40,48},{48,56},{56,6... | collective-permute-start | bytes 3538952 | tf_op jit(solution)/shard_map/ppermute | solution.py:297
  13.0 2.3 %collective-permute-start.4 = (bf16[18,64,512]{2,1,0:T(8,128)(2,1)}, bf16[18,64,512]{2,1,0:T(8,128)(2,1)}, u32[]{:S(2)}, u32[]{:S(2)}) collective-permute-start(bf16[18,64,512]{2,1,0:T(8,128)(2,1)} %get-tuple-element.28), channel_id=1, source_target_pairs={{128,120},{8,0},{16,8},{24,16},{32,24},{40,32},{48,40},{56,48},{64... | collective-permute-start | bytes 3538952 | tf_op jit(solution)/shard_map/ppermute | solution.py:297
  15.4 5.7 %shard_map.83 = (bf16[18,64,512]{2,1,0:T(8,128)(2,1)}, bf16[18,64,512]{2,1,0:T(8,128)(2,1)}, s32[1]{0:T(128)}) custom-call(s32[1]{0:T(128)} %get-tuple-element.23.flag_ref, s32[128,1]{1,0:T(8,128)} %copy.11.send_ref, bf16[18,256,1024]{2,1,0:T(8,128)(2,1)} %bitcast.24, bf16[18,256,1024]{2,1,0:T(8,128)(2,1)} %bitcast.25), custom_call_target="tpu_custom_call" | custom-call | flops 603979776 | bytes 7077888 | tf_op jit(solution)/shard_map/pallas_call | solution.py:65
  21.1 5.8 %collective-permute-start = (bf16[18,64,512]{2,1,0:T(8,128)(2,1)}, bf16[18,64,512]{2,1,0:T(8,128)(2,1)S(1)}, u32[]{:S(2)}, u32[]{:S(2)}) collective-permute-start(bf16[18,64,512]{2,1,0:T(8,128)(2,1)} %get-tuple-element.25), channel_id=1, source_target_pairs={{120,0},{0,8},{8,16},{16,24},{24,32},{32,40},{40,48},{48,56},{56,6... | collective-permute-start | bytes 3538952 | tf_op jit(solution)/shard_map/ppermute | solution.py:297
  26.9 1.4 collective-permute-start.1
  28.9 9.1 %collective-permute-done.3.below_ref = bf16[18,64,512]{2,1,0:T(8,128)(2,1)S(1)} collective-permute-done((bf16[18,64,512]{2,1,0:T(8,128)(2,1)}, bf16[18,64,512]{2,1,0:T(8,128)(2,1)S(1)}, u32[]{:S(2)}, u32[]{:S(2)}) %collective-permute-start.3) | collective-permute-done | bytes 1179680 | tf_op jit(solution)/shard_map/ppermute | solution.py:297
  38.0 1.3 collective-permute-done.4.above_ref
  39.3 1.3 broadcast_select_fusion
  40.5 1.3 collective-permute-start.5
  41.8 0.1 stack.35
  42.0 0.6 gather_fusion.1
  42.5 0.6 gather_fusion
  43.1 1.1 copy.16.second_ref
  44.1 1.0 copy.15.first_ref
  45.2 18.1 %collective-permute-done.below_ref = bf16[18,64,512]{2,1,0:T(8,128)(2,1)S(1)} collective-permute-done((bf16[18,64,512]{2,1,0:T(8,128)(2,1)}, bf16[18,64,512]{2,1,0:T(8,128)(2,1)S(1)}, u32[]{:S(2)}, u32[]{:S(2)}) %collective-permute-start) | collective-permute-done | bytes 1179680 | tf_op jit(solution)/shard_map/ppermute | solution.py:297
  63.2 1.3 collective-permute-done.1.above_ref
  64.5 0.1 broadcast_select_fusion.1
  64.7 0.9 copy-done.2
  65.6 1.3 collective-permute-start.2
  66.8 6.1 %collective-permute-done.5.relay_ref = bf16[18,64,512]{2,1,0:T(8,128)(2,1)} collective-permute-done((bf16[18,64,512]{2,1,0:T(8,128)(2,1)}, bf16[18,64,512]{2,1,0:T(8,128)(2,1)}, u32[]{:S(2)}, u32[]{:S(2)}) %collective-permute-start.5) | collective-permute-done | bytes 1179680 | tf_op jit(solution)/shard_map/ppermute | solution.py:307
  72.9 21.1 %shard_map.84 = (f32[512,512]{1,0:T(8,128)}, f32[512,512]{1,0:T(8,128)}) custom-call(s32[1]{0:T(128)} %get-tuple-element.24.flag_ref.token_ref, s32[1024,1]{1,0:T(8,128)} %copy.15.first_ref, s32[1024,1]{1,0:T(8,128)} %copy.16.second_ref, bf16[18,256,1024]{2,1,0:T(8,128)(2,1)} %bitcast.26, bf16[18,256,1024]{2,1,0:T(8,128)(2,1)} %bitcast.27, ...), custom_call_target="tpu_custom_call" | custom-call | flops 12079595520 | bytes 7077888 | tf_op jit(solution)/shard_map/pallas_call | solution.py:151
  94.0 5.0 %collective-permute-start.6 = (f32[512,512]{1,0:T(8,128)}, f32[512,512]{1,0:T(8,128)S(1)}, u32[]{:S(2)}, u32[]{:S(2)}) collective-permute-start(f32[512,512]{1,0:T(8,128)} %get-tuple-element.30), channel_id=1, source_target_pairs={{0,1},{1,0},{2,3},{3,2},{4,5},{5,4},{6,7},{7,6},{8,9},{9,8},{10,11... | collective-permute-start | bytes 3145736 | tf_op jit(solution)/shard_map/ppermute | solution.py:310
  99.0 2.5 %collective-permute-done.6.other_ref = f32[512,512]{1,0:T(8,128)S(1)} collective-permute-done((f32[512,512]{1,0:T(8,128)}, f32[512,512]{1,0:T(8,128)S(1)}, u32[]{:S(2)}, u32[]{:S(2)}) %collective-permute-start.6) | collective-permute-done | bytes 1048608 | tf_op jit(solution)/shard_map/ppermute | solution.py:310
  101.5 1.0 copy-done.5
  102.5 2.5 %shard_map.85 = (f32[128,512]{1,0:T(8,128)}, s16[144,512]{1,0:T(8,128)(2,1)}, s16[144,512]{1,0:T(8,128)(2,1)}, s16[144,512]{1,0:T(8,128)(2,1)}) custom-call(f32[512,512]{1,0:T(8,128)} %get-tuple-element.29.keep_ref.token_ref, f32[512,512]{1,0:T(8,128)} %copy-done.5, f32[512,512]{1,0:T(8,128)} %get-tuple-element.29.keep_ref.token_ref), custom_call_target="tpu_custom_call" | custom-call | tf_op jit(solution)/shard_map/pallas_call | solution.py:200
  105.0 0.0 collective-permute-done.2.relay_ref
  105.1 20.6 %shard_map.86 = (f32[512,512]{1,0:T(8,128)}, f32[512,512]{1,0:T(8,128)}) custom-call(s32[1]{0:T(128)} %get-tuple-element.24.flag_ref.token_ref, s32[1024,1]{1,0:T(8,128)} %copy.15.first_ref, s32[1024,1]{1,0:T(8,128)} %copy.16.second_ref, bf16[18,256,1024]{2,1,0:T(8,128)(2,1)} %bitcast.28, bf16[18,256,1024]{2,1,0:T(8,128)(2,1)} %bitcast.29, ...), custom_call_target="tpu_custom_call" | custom-call | flops 12079595520 | bytes 7077888 | tf_op jit(solution)/shard_map/pallas_call | solution.py:151
  125.7 0.4 collective-permute-start.7
  126.1 0.7 collective-permute-start.11
  126.8 0.0 collective-permute-start.12
  126.8 1.9 %collective-permute-start.13 = (s16[144,512]{1,0:T(8,128)(2,1)S(1)}, s16[144,512]{1,0:T(8,128)(2,1)S(1)}, u32[]{:S(2)}, u32[]{:S(2)}) collective-permute-start(s16[144,512]{1,0:T(8,128)(2,1)S(1)} %copy-done.13), channel_id=1, source_target_pairs={{0,6},{1,7},{2,4},{3,5},{4,2},{5,3},{6,0},{7,1},{8,14},{9,15},{10,... | collective-permute-start | bytes 442376 | tf_op jit(solution)/shard_map/ppermute | solution.py:314
  128.7 0.0 collective-permute-done.7.other_ref
  128.7 1.0 copy-done.4
  129.7 2.6 %shard_map.87 = (f32[128,512]{1,0:T(8,128)}, s16[144,512]{1,0:T(8,128)(2,1)}, s16[144,512]{1,0:T(8,128)(2,1)}, s16[144,512]{1,0:T(8,128)(2,1)}) custom-call(f32[512,512]{1,0:T(8,128)} %get-tuple-element.32.keep_ref.token_ref, f32[512,512]{1,0:T(8,128)} %copy-done.4, f32[512,512]{1,0:T(8,128)} %get-tuple-element.32.keep_ref.token_ref), custom_call_target="tpu_custom_call" | custom-call | tf_op jit(solution)/shard_map/pallas_call | solution.py:200
  132.3 1.6 %collective-permute-start.8 = (s16[144,512]{1,0:T(8,128)(2,1)}, s16[144,512]{1,0:T(8,128)(2,1)S(1)}, u32[]{:S(2)}, u32[]{:S(2)}) collective-permute-start(s16[144,512]{1,0:T(8,128)(2,1)} %get-tuple-element.35), channel_id=1, source_target_pairs={{0,2},{1,3},{2,0},{3,1},{4,6},{5,7},{6,4},{7,5},{8,10},{9,11},{10,... | collective-permute-start | bytes 442376 | tf_op jit(solution)/shard_map/ppermute | solution.py:314
  133.9 0.0 collective-permute-start.9
  133.9 0.0 collective-permute-done.11.refs_1_
  133.9 1.2 collective-permute-start.10
  135.1 13.3 %collective-permute-done.13.refs_3_ = s16[144,512]{1,0:T(8,128)(2,1)S(1)} collective-permute-done((s16[144,512]{1,0:T(8,128)(2,1)S(1)}, s16[144,512]{1,0:T(8,128)(2,1)S(1)}, u32[]{:S(2)}, u32[]{:S(2)}) %collective-permute-start.13) | collective-permute-done | bytes 147488 | tf_op jit(solution)/shard_map/ppermute | solution.py:314
  148.4 0.7 copy-done.9
  149.1 3.6 %shard_map.88.refs_4_ = f32[1001,128]{1,0:T(8,128)} custom-call(bf16[1001,512]{1,0:T(8,128)(2,1)} %constant.44.clone.coarse_ref, bf16[1001,512]{1,0:T(8,128)(2,1)} %constant.45.clone.fine_ref, f32[128,512]{1,0:T(8,128)} %get-tuple-element.31.token_ref.refs_0_, s16[144,512]{1,0:T(8,128)(2,1)} %copy-done.7, s16[144,512]{1,0:T(8,128)(2,1)} %copy-done.8, ...), custom_call_target="tpu_custom_call" | custom-call | tf_op jit(solution)/shard_map/pallas_call | solution.py:237
  152.7 0.0 collective-permute-done.8.refs_1_
  152.7 0.0 collective-permute-done.9.refs_2_
  152.7 2.1 %collective-permute-done.10.refs_3_ = s16[144,512]{1,0:T(8,128)(2,1)S(1)} collective-permute-done((s16[144,512]{1,0:T(8,128)(2,1)}, s16[144,512]{1,0:T(8,128)(2,1)S(1)}, u32[]{:S(2)}, u32[]{:S(2)}) %collective-permute-start.10) | collective-permute-done | bytes 147488 | tf_op jit(solution)/shard_map/ppermute | solution.py:314
  154.8 0.7 copy-done.12
  155.4 3.8 %shard_map.89 = f32[1001,128]{1,0:T(8,128)} custom-call(bf16[1001,512]{1,0:T(8,128)(2,1)} %constant.46.clone.coarse_ref, bf16[1001,512]{1,0:T(8,128)(2,1)} %constant.47.clone.fine_ref, f32[128,512]{1,0:T(8,128)} %get-tuple-element.34.refs_0_, s16[144,512]{1,0:T(8,128)(2,1)} %copy-done.10, s16[144,512]{1,0:T(8,128)(2,1)} %copy-done.11, ...), custom_call_target="tpu_custom_call" | custom-call | tf_op jit(solution)/shard_map/pallas_call | solution.py:237
  (30 shorter events, 0.1 us)
Async XLA Ops:
  0.0 41.9 %copy-start = (s32[1024]{0:T(1024)S(1)}, s32[1024]{0:T(1024)}, u32[]{:S(2)}) copy-start(s32[1024]{0:T(1024)} %param.11) | copy-start | bytes 12292
  6.4 31.5 %collective-permute-start.3 = (bf16[18,64,512]{2,1,0:T(8,128)(2,1)}, bf16[18,64,512]{2,1,0:T(8,128)(2,1)S(1)}, u32[]{:S(2)}, u32[]{:S(2)}) collective-permute-start(bf16[18,64,512]{2,1,0:T(8,128)(2,1)} %get-tuple-element.27), channel_id=1, source_target_pairs={{120,0},{0,8},{8,16},{16,24},{24,32},{32,40},{40,48},{48,56},{56,6... | collective-permute-start | bytes 3538952 | tf_op jit(solution)/shard_map/ppermute | solution.py:297
  13.0 26.2 %collective-permute-start.4 = (bf16[18,64,512]{2,1,0:T(8,128)(2,1)}, bf16[18,64,512]{2,1,0:T(8,128)(2,1)}, u32[]{:S(2)}, u32[]{:S(2)}) collective-permute-start(bf16[18,64,512]{2,1,0:T(8,128)(2,1)} %get-tuple-element.28), channel_id=1, source_target_pairs={{128,120},{8,0},{16,8},{24,16},{32,24},{40,32},{48,40},{56,48},{64... | collective-permute-start | bytes 3538952 | tf_op jit(solution)/shard_map/ppermute | solution.py:297
  21.1 42.2 %collective-permute-start = (bf16[18,64,512]{2,1,0:T(8,128)(2,1)}, bf16[18,64,512]{2,1,0:T(8,128)(2,1)S(1)}, u32[]{:S(2)}, u32[]{:S(2)}) collective-permute-start(bf16[18,64,512]{2,1,0:T(8,128)(2,1)} %get-tuple-element.25), channel_id=1, source_target_pairs={{120,0},{0,8},{8,16},{16,24},{24,32},{32,40},{40,48},{48,56},{56,6... | collective-permute-start | bytes 3538952 | tf_op jit(solution)/shard_map/ppermute | solution.py:297
  26.9 37.6 %collective-permute-start.1 = (bf16[18,64,512]{2,1,0:T(8,128)(2,1)}, bf16[18,64,512]{2,1,0:T(8,128)(2,1)S(1)}, u32[]{:S(2)}, u32[]{:S(2)}) collective-permute-start(bf16[18,64,512]{2,1,0:T(8,128)(2,1)} %get-tuple-element.26), channel_id=1, source_target_pairs={{128,120},{8,0},{16,8},{24,16},{32,24},{40,32},{48,40},{56,48},{64... | collective-permute-start | bytes 3538952 | tf_op jit(solution)/shard_map/ppermute | solution.py:297
  38.0 2.6 %copy-start.3 = (bf16[18,64,512]{2,1,0:T(8,128)(2,1)}, bf16[18,64,512]{2,1,0:T(8,128)(2,1)S(1)}, u32[]{:S(2)}) copy-start(bf16[18,64,512]{2,1,0:T(8,128)(2,1)S(1)} %collective-permute-done.3.below_ref) | copy-start | bytes 3538948
  39.3 3.3 %copy-start.6 = (s32[1024]{0:T(1024)S(1)}, s32[1024]{0:T(1024)}, u32[]{:S(2)}) copy-start(s32[1024]{0:T(1024)} %param.10) | copy-start | bytes 12292
  40.5 32.4 %collective-permute-start.5 = (bf16[18,64,512]{2,1,0:T(8,128)(2,1)}, bf16[18,64,512]{2,1,0:T(8,128)(2,1)}, u32[]{:S(2)}, u32[]{:S(2)}) collective-permute-start(bf16[18,64,512]{2,1,0:T(8,128)(2,1)} %broadcast_select_fusion), channel_id=1, source_target_pairs={{0,128},{1,129},{2,130},{3,131},{252,124},{253,125},{254,126},{255... | collective-permute-start | bytes 3538952 | tf_op jit(solution)/shard_map/ppermute | solution.py:307
  63.2 1.4 copy-start.1
  64.5 1.0 copy-start.2
  65.6 39.5 %collective-permute-start.2 = (bf16[18,64,512]{2,1,0:T(8,128)(2,1)S(1)}, bf16[18,64,512]{2,1,0:T(8,128)(2,1)}, u32[]{:S(2)}, u32[]{:S(2)}) collective-permute-start(bf16[18,64,512]{2,1,0:T(8,128)(2,1)S(1)} %broadcast_select_fusion.1), channel_id=1, source_target_pairs={{0,128},{1,129},{2,130},{3,131},{252,124},{253,125},{254,126},{255... | collective-permute-start | bytes 3538952 | tf_op jit(solution)/shard_map/ppermute | solution.py:307
  94.0 7.5 %collective-permute-start.6 = (f32[512,512]{1,0:T(8,128)}, f32[512,512]{1,0:T(8,128)S(1)}, u32[]{:S(2)}, u32[]{:S(2)}) collective-permute-start(f32[512,512]{1,0:T(8,128)} %get-tuple-element.30), channel_id=1, source_target_pairs={{0,1},{1,0},{2,3},{3,2},{4,5},{5,4},{6,7},{7,6},{8,9},{9,8},{10,11... | collective-permute-start | bytes 3145736 | tf_op jit(solution)/shard_map/ppermute | solution.py:310
  101.5 1.0 copy-start.5
  105.0 21.0 %copy-start.15 = (s16[144,512]{1,0:T(8,128)(2,1)S(1)}, s16[144,512]{1,0:T(8,128)(2,1)}, u32[]{:S(2)}) copy-start(s16[144,512]{1,0:T(8,128)(2,1)} %get-tuple-element.38) | copy-start | bytes 442372
  105.0 21.8 %copy-start.14 = (s16[144,512]{1,0:T(8,128)(2,1)S(1)}, s16[144,512]{1,0:T(8,128)(2,1)}, u32[]{:S(2)}) copy-start(s16[144,512]{1,0:T(8,128)(2,1)} %get-tuple-element.39) | copy-start | bytes 442372
  105.0 21.8 %copy-start.13 = (s16[144,512]{1,0:T(8,128)(2,1)S(1)}, s16[144,512]{1,0:T(8,128)(2,1)}, u32[]{:S(2)}) copy-start(s16[144,512]{1,0:T(8,128)(2,1)} %get-tuple-element.40) | copy-start | bytes 442372
  125.7 3.0 %collective-permute-start.7 = (f32[512,512]{1,0:T(8,128)}, f32[512,512]{1,0:T(8,128)S(1)}, u32[]{:S(2)}, u32[]{:S(2)}) collective-permute-start(f32[512,512]{1,0:T(8,128)} %get-tuple-element.33), channel_id=1, source_target_pairs={{0,1},{1,0},{2,3},{3,2},{4,5},{5,4},{6,7},{7,6},{8,9},{9,8},{10,11... | collective-permute-start | bytes 3145736 | tf_op jit(solution)/shard_map/ppermute | solution.py:310
  126.1 7.8 %collective-permute-start.11 = (s16[144,512]{1,0:T(8,128)(2,1)S(1)}, s16[144,512]{1,0:T(8,128)(2,1)S(1)}, u32[]{:S(2)}, u32[]{:S(2)}) collective-permute-start(s16[144,512]{1,0:T(8,128)(2,1)S(1)} %copy-done.15), channel_id=1, source_target_pairs={{0,2},{1,3},{2,0},{3,1},{4,6},{5,7},{6,4},{7,5},{8,10},{9,11},{10,... | collective-permute-start | bytes 442376 | tf_op jit(solution)/shard_map/ppermute | solution.py:314
  126.8 8.3 %collective-permute-start.12 = (s16[144,512]{1,0:T(8,128)(2,1)S(1)}, s16[144,512]{1,0:T(8,128)(2,1)S(1)}, u32[]{:S(2)}, u32[]{:S(2)}) collective-permute-start(s16[144,512]{1,0:T(8,128)(2,1)S(1)} %copy-done.14), channel_id=1, source_target_pairs={{0,4},{1,5},{2,6},{3,7},{4,0},{5,1},{6,2},{7,3},{8,12},{9,13},{10,... | collective-permute-start | bytes 442376 | tf_op jit(solution)/shard_map/ppermute | solution.py:314
  126.8 21.6 %collective-permute-start.13 = (s16[144,512]{1,0:T(8,128)(2,1)S(1)}, s16[144,512]{1,0:T(8,128)(2,1)S(1)}, u32[]{:S(2)}, u32[]{:S(2)}) collective-permute-start(s16[144,512]{1,0:T(8,128)(2,1)S(1)} %copy-done.13), channel_id=1, source_target_pairs={{0,6},{1,7},{2,4},{3,5},{4,2},{5,3},{6,0},{7,1},{8,14},{9,15},{10,... | collective-permute-start | bytes 442376 | tf_op jit(solution)/shard_map/ppermute | solution.py:314
  128.7 1.0 copy-start.4
  132.3 20.4 %collective-permute-start.8 = (s16[144,512]{1,0:T(8,128)(2,1)}, s16[144,512]{1,0:T(8,128)(2,1)S(1)}, u32[]{:S(2)}, u32[]{:S(2)}) collective-permute-start(s16[144,512]{1,0:T(8,128)(2,1)} %get-tuple-element.35), channel_id=1, source_target_pairs={{0,2},{1,3},{2,0},{3,1},{4,6},{5,7},{6,4},{7,5},{8,10},{9,11},{10,... | collective-permute-start | bytes 442376 | tf_op jit(solution)/shard_map/ppermute | solution.py:314
  133.9 18.8 %collective-permute-start.9 = (s16[144,512]{1,0:T(8,128)(2,1)}, s16[144,512]{1,0:T(8,128)(2,1)S(1)}, u32[]{:S(2)}, u32[]{:S(2)}) collective-permute-start(s16[144,512]{1,0:T(8,128)(2,1)} %get-tuple-element.36), channel_id=1, source_target_pairs={{0,4},{1,5},{2,6},{3,7},{4,0},{5,1},{6,2},{7,3},{8,12},{9,13},{10,... | collective-permute-start | bytes 442376 | tf_op jit(solution)/shard_map/ppermute | solution.py:314
  133.9 14.5 %copy-start.7 = (s16[144,512]{1,0:T(8,128)(2,1)}, s16[144,512]{1,0:T(8,128)(2,1)S(1)}, u32[]{:S(2)}) copy-start(s16[144,512]{1,0:T(8,128)(2,1)S(1)} %collective-permute-done.11.refs_1_) | copy-start | bytes 442372
  133.9 20.8 %collective-permute-start.10 = (s16[144,512]{1,0:T(8,128)(2,1)}, s16[144,512]{1,0:T(8,128)(2,1)S(1)}, u32[]{:S(2)}, u32[]{:S(2)}) collective-permute-start(s16[144,512]{1,0:T(8,128)(2,1)} %get-tuple-element.37), channel_id=1, source_target_pairs={{0,6},{1,7},{2,4},{3,5},{4,2},{5,3},{6,0},{7,1},{8,14},{9,15},{10,... | collective-permute-start | bytes 442376 | tf_op jit(solution)/shard_map/ppermute | solution.py:314
  135.1 13.3 %copy-start.8 = (s16[144,512]{1,0:T(8,128)(2,1)}, s16[144,512]{1,0:T(8,128)(2,1)S(1)}, u32[]{:S(2)}) copy-start(s16[144,512]{1,0:T(8,128)(2,1)S(1)} %collective-permute-done.12.refs_2_) | copy-start | bytes 442372
  148.4 0.7 copy-start.9
  152.7 2.1 %copy-start.10 = (s16[144,512]{1,0:T(8,128)(2,1)}, s16[144,512]{1,0:T(8,128)(2,1)S(1)}, u32[]{:S(2)}) copy-start(s16[144,512]{1,0:T(8,128)(2,1)S(1)} %collective-permute-done.8.refs_1_) | copy-start | bytes 442372
  152.7 2.1 %copy-start.11 = (s16[144,512]{1,0:T(8,128)(2,1)}, s16[144,512]{1,0:T(8,128)(2,1)S(1)}, u32[]{:S(2)}) copy-start(s16[144,512]{1,0:T(8,128)(2,1)S(1)} %collective-permute-done.9.refs_2_) | copy-start | bytes 442372
  154.8 0.7 copy-start.12

commit v2 on v1

v2 whole, which is shorter than its diff:
```python
import functools

import jax
import jax.numpy as jnp
import numpy as np
from jax import lax
from jax.experimental import pallas as pl
from jax.experimental.pallas import tpu as pltpu
from jax.sharding import PartitionSpec as P

HALF_LAG = 500
LANES = 128
CHUNKS = ((0, 1), (2, 3))
PIECE = 32
SEG_STEP = 9
VMEM = 60 << 20
SCALE_ROWS = 16
TOP = 32000.0


def one_hot(ids, width, base):
    slots = lax.broadcasted_iota(jnp.int32, (ids.shape[0], width), 1) + base
    return (ids == slots).astype(jnp.float32).astype(jnp.bfloat16)


def anywhere():
    return pl.BlockSpec(memory_space=pl.ANY)


def scalars():
    return pl.BlockSpec(memory_space=pltpu.SMEM)


def params():
    return pltpu.CompilerParams(vmem_limit_bytes=VMEM)


def border_kernel(flag_ref, send_ref, real_ref, imag_ref, below_ref, above_ref, next_ref, pick_ref):
    next_ref[0] = flag_ref[0]
    next_ref[1] = flag_ref[1]

    @pl.when((pl.program_id(0) == 0) & (pl.program_id(1) == 0))
    def _():
        pick_ref[...] = one_hot(send_ref[...], pick_ref.shape[1], 0)

    half = below_ref.shape[1]
    step = real_ref.shape[0]
    for seg in range(step):
        rows = jnp.concatenate([real_ref[seg], imag_ref[seg]], axis=1)
        lent = jnp.dot(pick_ref[...], rows, preferred_element_type=jnp.float32)
        lent = lent.astype(jnp.bfloat16)
        below_ref[seg] = lent[:half]
        above_ref[seg] = lent[half:]


def lent_rows(flags, spectra, send_list, chunk):
    groups, stations, width = spectra.shape
    count = send_list.shape[0]
    half = count // 2
    first, blocks = chunk[0], len(chunk)
    offset = width // 2 // LANES
    step = 9
    lanes = 2 * LANES * blocks
    out = jax.ShapeDtypeStruct((groups, half, lanes), jnp.bfloat16)
    out_spec = pl.BlockSpec((step, half, 2 * LANES), lambda j, g: (g, 0, j))
    return pl.pallas_call(
        border_kernel,
        grid=(blocks, groups // step),
        in_specs=[
            scalars(),
            pl.BlockSpec((count, 1), lambda j, g: (0, 0)),
            pl.BlockSpec((step, stations, LANES), lambda j, g: (g, 0, first + j)),
            pl.BlockSpec((step, stations, LANES), lambda j, g: (g, 0, first + j + offset)),
        ],
        out_specs=[out_spec, out_spec, scalars()],
        out_shape=[out, out, jax.ShapeDtypeStruct((2,), jnp.int32)],
        scratch_shapes=[pltpu.VMEM((count, stations), jnp.bfloat16)],
        compiler_params=params(),
    )(flags, send_list.reshape(count, 1), spectra, spectra)


def prepare_kernel(
    flag_ref, first_ref, second_ref, own_ref, halo_ref, sort_ref, kind_ref, next_ref, place_ref
):
    next_ref[0] = flag_ref[0]
    next_ref[1] = flag_ref[1]
    me = flag_ref[1]
    members, kept = first_ref.shape
    stations = own_ref.shape[2]
    size = halo_ref.shape[1]

    needs = second_ref[...] >= stations
    marks = needs.astype(jnp.float32)
    rows = lax.broadcasted_iota(jnp.int32, (kept, kept), 0)
    columns = lax.broadcasted_iota(jnp.int32, (kept, kept), 1)
    earlier = (rows < columns).astype(jnp.float32).astype(jnp.bfloat16)
    before = jnp.dot(marks.astype(jnp.bfloat16), earlier, preferred_element_type=jnp.float32)
    count = jnp.sum(marks, axis=1, keepdims=True)
    position = lax.broadcasted_iota(jnp.int32, (members, kept), 1).astype(jnp.float32)
    place = jnp.where(needs, before, count + position - before)
    place_ref[...] = place.astype(jnp.int32)
    most, least = jnp.max(count), jnp.min(count)
    pieces = own_ref.shape[0]
    for piece in range(pieces):
        kind_ref[piece] = (most > piece * PIECE).astype(jnp.int32)
        kind_ref[pieces + piece] = (least < (piece + 1) * PIECE).astype(jnp.int32)

    def choose(ids, width, base):
        slots = lax.broadcasted_iota(jnp.int32, (width, kept), 0) + base
        return (ids == slots).astype(jnp.float32).astype(jnp.bfloat16)

    dims = (((1,), (1,)), ((), ()))
    for slot in range(members):
        half = members // 2
        block = me ^ (2 * slot + 1 if slot < half else 2 * (slot - half))
        row = pl.ds(block, 1)
        sort = choose(place_ref[row, :], kept, 0)
        if slot == half:
            sort_ref[...] = sort
        first, second = first_ref[row, :], second_ref[row, :]
        picks = [choose(first, stations, 0), choose(second, stations, 0), choose(second, halo_ref.shape[2], stations)]
        a, b, c = [
            lax.dot_general(sort, pick, dims, preferred_element_type=jnp.float32).astype(jnp.bfloat16)
            for pick in picks
        ]
        for piece in range(pieces):
            part = slice(piece * PIECE, (piece + 1) * PIECE)
            start = slot * PIECE
            own_ref[piece, start : start + PIECE] = a[part]
            own_ref[piece, size + start : size + start + PIECE] = b[part]
            halo_ref[piece, start : start + PIECE] = c[part]


def prepare(flags, first_ids, second_ids, stations, lent):
    members, kept = first_ids.shape
    pieces, size = kept // PIECE, members * PIECE
    whole = pl.BlockSpec(memory_space=pltpu.VMEM)
    return pl.pallas_call(
        prepare_kernel,
        in_specs=[scalars(), whole, whole],
        out_specs=[whole, whole, whole, scalars(), scalars()],
        out_shape=[
            jax.ShapeDtypeStruct((pieces, 2 * size, stations), jnp.bfloat16),
            jax.ShapeDtypeStruct((pieces, size, 2 * lent), jnp.bfloat16),
            jax.ShapeDtypeStruct((kept, kept), jnp.bfloat16),
            jax.ShapeDtypeStruct((2 * pieces,), jnp.int32),
            jax.ShapeDtypeStruct((2,), jnp.int32),
        ],
        scratch_shapes=[pltpu.VMEM((members, kept), jnp.int32)],
        compiler_params=params(),
    )(flags, first_ids, second_ids)


def add_products(a, b, sums):
    ar, ai, br, bi = a[:, :LANES], a[:, LANES:], b[:, :LANES], b[:, LANES:]
    real, imag = sums
    return real + (ar * br + ai * bi), imag + (ai * br - ar * bi)


def spots(out_refs, kept, piece):
    return [
        (ref, slice(start + piece * PIECE, start + (piece + 1) * PIECE))
        for ref in out_refs
        for start in range(0, ref.shape[0], kept)
    ]


def read_sums(out_refs, kept, piece):
    rows = jnp.concatenate([ref[part] for ref, part in spots(out_refs, kept, piece)], axis=0)
    return rows[:, :LANES], rows[:, LANES:]


def write_sums(out_refs, kept, piece, sums):
    rows = jnp.concatenate(sums, axis=1)
    for place, (ref, part) in enumerate(spots(out_refs, kept, piece)):
        ref[part] = rows[place * PIECE : (place + 1) * PIECE]


def own_kernel(flag_ref, kind_ref, own_ref, real_ref, imag_ref, send_ref, keep_ref, next_ref):
    next_ref[0] = flag_ref[0]
    next_ref[1] = flag_ref[1]
    pieces = own_ref.shape[0]
    size = own_ref.shape[1] // 2
    kept = pieces * PIECE
    outs = (send_ref, keep_ref)

    @pl.when(pl.program_id(1) == 0)
    def _():
        send_ref[...] = jnp.zeros_like(send_ref)
        keep_ref[...] = jnp.zeros_like(keep_ref)

    for piece in range(pieces):

        @pl.when(kind_ref[piece] == 0)
        def _():
            sums = read_sums(outs, kept, piece)
            for seg in range(real_ref.shape[0]):
                table = jnp.concatenate([real_ref[seg], imag_ref[seg]], axis=1)
                both = jnp.dot(own_ref[piece], table, preferred_element_type=jnp.float32)
                sums = add_products(both[:size], both[size:], sums)
            write_sums(outs, kept, piece, sums)


def own_cross(flags, kinds, own, spectra, pairs):
    groups, stations, width = spectra.shape
    blocks = width // 2 // LANES
    out = jax.ShapeDtypeStruct((pairs // 2, width), jnp.float32)
    return pl.pallas_call(
        own_kernel,
        grid=(blocks, groups // SEG_STEP),
        in_specs=[
            scalars(),
            scalars(),
            pl.BlockSpec(own.shape, lambda j, g: (0, 0, 0)),
            pl.BlockSpec((SEG_STEP, stations, LANES), lambda j, g: (g, 0, j)),
            pl.BlockSpec((SEG_STEP, stations, LANES), lambda j, g: (g, 0, j + blocks)),
        ],
        out_specs=[pl.BlockSpec((pairs // 2, 2 * LANES), lambda j, g: (0, j))] * 2 + [scalars()],
        out_shape=[out, out, jax.ShapeDtypeStruct((2,), jnp.int32)],
        compiler_params=params(),
    )(flags, kinds, own, spectra, spectra)


def cross_kernel(
    flag_ref, kind_ref, own_ref, halo_ref, real_ref, imag_ref, first_send_ref, first_keep_ref,
    below_ref, above_ref, relay_ref, token_ref, near_ref, far_ref, keep_ref, border_ref,
):
    lent = below_ref.shape[1]
    pieces, size = halo_ref.shape[:2]
    kept = pieces * PIECE
    groups = real_ref.shape[0]
    outs = (near_ref, far_ref, keep_ref)
    cut = near_ref.shape[0]

    @pl.when(pl.program_id(1) == 0)
    def _():
        near_ref[...] = first_send_ref[:cut]
        far_ref[...] = first_send_ref[cut:]
        keep_ref[...] = first_keep_ref[...]

    border_ref[:, :lent] = below_ref[...]
    border_ref[:, lent:] = above_ref[...]

    @pl.when(flag_ref[0] == 1)
    def _():
        border_ref[:, :lent] = relay_ref[...]

    @pl.when(flag_ref[0] == 2)
    def _():
        border_ref[:, lent:] = relay_ref[...]

    def add(piece, mixed):
        sums = read_sums(outs, kept, piece)
        for seg in range(groups):
            table = jnp.concatenate([real_ref[seg], imag_ref[seg]], axis=1)
            rows = own_ref[piece] if mixed else own_ref[piece, :size]
            gathered = jnp.dot(rows, table, preferred_element_type=jnp.float32)
            b = jnp.dot(halo_ref[piece], border_ref[seg], preferred_element_type=jnp.float32)
            if mixed:
                b = b + gathered[size:]
            sums = add_products(gathered[:size], b, sums)
        write_sums(outs, kept, piece, sums)

    for piece in range(pieces):
        needed, mixed = kind_ref[piece] == 1, kind_ref[pieces + piece] == 1

        @pl.when(needed & mixed)
        def _():
            add(piece, True)

        @pl.when(needed & jnp.logical_not(mixed))
        def _():
            add(piece, False)


def pair_cross(flags, kinds, own, picks, spectra, firsts, halo, chunk, token):
    groups, stations, width = spectra.shape
    lent = halo[0].shape[1]
    half_pairs = firsts[0].shape[0]
    offset = width // 2 // LANES
    first, parts = chunk[0], len(chunk)
    halo_spec = pl.BlockSpec((SEG_STEP, lent, 2 * LANES), lambda j, g: (g, 0, j))
    first_spec = pl.BlockSpec((half_pairs, 2 * LANES), lambda j, g: (0, first + j))
    heights = (half_pairs // 2, half_pairs // 2, half_pairs)
    return pl.pallas_call(
        cross_kernel,
        grid=(parts, groups // SEG_STEP),
        in_specs=[
            scalars(),
            scalars(),
            pl.BlockSpec(own.shape, lambda j, g: (0, 0, 0)),
            pl.BlockSpec(picks.shape, lambda j, g: (0, 0, 0)),
            pl.BlockSpec((SEG_STEP, stations, LANES), lambda j, g: (g, 0, first + j)),
            pl.BlockSpec((SEG_STEP, stations, LANES), lambda j, g: (g, 0, first + j + offset)),
            first_spec,
            first_spec,
            halo_spec,
            halo_spec,
            halo_spec,
            anywhere(),
        ],
        out_specs=[pl.BlockSpec((height, 2 * LANES), lambda j, g: (0, j)) for height in heights],
        out_shape=[jax.ShapeDtypeStruct((height, 2 * LANES * parts), jnp.float32) for height in heights],
        scratch_shapes=[pltpu.VMEM((SEG_STEP, 2 * lent, 2 * LANES), jnp.bfloat16)],
        compiler_params=params(),
    )(flags, kinds, own, picks, spectra, spectra, *firsts, *halo, token)


def pack_kernel(keep_ref, near_ref, far_ref, token_ref, own_ref, *out_refs):
    kept = own_ref.shape[0]
    cut = near_ref.shape[0]
    own_ref[...] = keep_ref[:kept] + near_ref[:kept]
    for k, out_ref in enumerate(out_refs, 1):
        rows = slice(k * kept, (k + 1) * kept)
        other = near_ref[rows] if rows.stop <= cut else far_ref[rows.start - cut : rows.stop - cut]
        total = keep_ref[rows] + other
        peak = jnp.max(jnp.abs(total), axis=0, keepdims=True)
        power = jnp.ceil(jnp.log2(jnp.maximum(peak, 1e-36) * 1.0001))
        scaled = jnp.round(total * jnp.exp2(-power) * TOP)
        out_ref[:kept] = scaled.astype(jnp.int32).astype(jnp.int16)
        powers = jnp.broadcast_to(power, (SCALE_ROWS, power.shape[1]))
        out_ref[kept:] = powers.astype(jnp.int32).astype(jnp.int16)


def pack(keep, near, far, token, parts):
    rows, lanes = keep.shape
    kept = rows // parts
    coded = jax.ShapeDtypeStruct((kept + SCALE_ROWS, lanes), jnp.int16)
    whole = pl.BlockSpec(memory_space=pltpu.VMEM)
    return pl.pallas_call(
        pack_kernel,
        in_specs=[whole, whole, whole, anywhere()],
        out_specs=[whole] * parts,
        out_shape=[jax.ShapeDtypeStruct((kept, lanes), jnp.float32)] + [coded] * (parts - 1),
        compiler_params=params(),
        cost_estimate=pl.CostEstimate(flops=1, bytes_accessed=1, transcendentals=0),
    )(keep, near, far, token)


def unpack(ref, kept):
    power = ref[kept:].astype(jnp.int32).astype(jnp.float32)[:1]
    return ref[:kept].astype(jnp.int32).astype(jnp.float32) * (1.0 / TOP) * jnp.exp2(power)


def lag_kernel(parts, has_base, coarse_ref, fine_ref, sort_ref, *refs):
    out_ref = refs[-1]
    kept = refs[0].shape[0]
    cross = refs[0][...]
    for ref in refs[1:parts]:
        cross = cross + unpack(ref, kept)

    def dot(left, right, axis):
        dims = (((axis,), (axis,)), ((), ()))
        return lax.dot_general(left, right, dims, preferred_element_type=jnp.float32)

    high = cross.astype(jnp.bfloat16)
    low = (cross - high.astype(jnp.float32)).astype(jnp.bfloat16)
    high = dot(sort_ref[...], high, 0).astype(jnp.bfloat16)
    low = dot(sort_ref[...], low, 0).astype(jnp.bfloat16)
    coarse = coarse_ref[...]
    lags = (dot(fine_ref[...], high, 1) + dot(coarse, low, 1)) + dot(coarse, high, 1)
    if has_base:
        lags = lags + refs[parts][...]
    out_ref[...] = lags


def lag_sums(tables, sort, total, base, token):
    operands = [*tables, sort, *total] + ([] if base is None else [base])
    specs = [pl.BlockSpec(memory_space=pltpu.VMEM)] * len(operands)
    if token is not None:
        operands.append(token)
        specs.append(anywhere())
    return pl.pallas_call(
        functools.partial(lag_kernel, len(total), int(base is not None)),
        in_specs=specs,
        out_shape=jax.ShapeDtypeStruct((2 * HALF_LAG + 1, total[0].shape[0]), jnp.float32),
        compiler_params=params(),
        cost_estimate=pl.CostEstimate(flops=10**11, bytes_accessed=10**9, transcendentals=0),
    )(*operands)


def lag_tables(freq_bins, blocks, scale):
    lags = np.arange(2 * HALF_LAG + 1)[:, None] - HALF_LAG
    columns = []
    for block in blocks:
        bins = np.arange(block * LANES, (block + 1) * LANES)[None, :]
        angles = (bins * lags % (2 * freq_bins)) * (np.pi / freq_bins)
        columns += [np.cos(angles), -np.sin(angles)]
    table = (np.concatenate(columns, axis=1) * scale).astype(np.float32)
    coarse = table.astype(jnp.bfloat16)
    fine = (table - coarse.astype(np.float32)).astype(jnp.bfloat16)
    return jnp.asarray(coarse), jnp.asarray(fine)


def per_device(spectra, send_list, pair_first, pair_second):
    stations, days, segs, width = spectra.shape
    members = lax.axis_size("day")
    tiles = lax.axis_size("tile")
    me = lax.axis_index("day")
    tile = lax.axis_index("tile")
    groups = days * segs
    pairs = pair_first.shape[0]
    kept = pairs // members
    flat = jnp.transpose(spectra, (1, 2, 0, 3)).reshape(groups, stations, width)

    middle, last = tiles // 2, tiles - 1

    def shift(ahead):
        source, target, end = (middle - 1, middle, 0) if ahead else (middle, middle - 1, last)
        pairs = []
        for d in range(members):
            straight = (d >= members // 2) == ahead
            pairs.append((source * members + d, (target if straight else end) * members + d))
            for t in range(tiles - 1):
                if t + 1 != middle:
                    low, high = t * members + d, (t + 1) * members + d
                    pairs.append((low, high) if ahead else (high, low))
        return pairs

    upward, downward = shift(True), shift(False)
    onward = [(d, middle * members + d) for d in range(members // 2)]
    onward += [(last * members + d, (middle - 1) * members + d) for d in range(members // 2, members)]
    both = ("tile", "day")
    side = jnp.where((tile == middle) & (me < members // 2), 1, 0)
    side = jnp.where((tile == middle - 1) & (me >= members // 2), 2, side)
    side = jnp.where(tile == last, 3, side)
    flags = jnp.stack([side.astype(jnp.int32), me.astype(jnp.int32)])

    def swap(k):
        return [(i, i ^ k) for i in range(members)]

    sent = []
    for chunk in CHUNKS:
        to_below, to_above, flags = lent_rows(flags, flat, send_list, chunk)
        sent.append((lax.ppermute(to_above, both, upward), lax.ppermute(to_below, both, downward)))

    half = members // 2
    shape = (members, kept)
    own, picks, sort, kinds, flags = prepare(
        flags, pair_first.reshape(shape), pair_second.reshape(shape), stations, send_list.shape[0] // 2
    )
    *firsts, after_own = own_cross(flags, kinds, own, flat, pairs)

    scale = 1.0 / np.sqrt(width * segs * days * members)
    lags = waiting = None
    gates = [flags] + [after_own] * (len(sent) - 1)
    passing = [
        jnp.where(gate[0] == 3, above, below) for gate, (below, above) in zip(gates, sent)
    ]
    token = passing[-1]
    for chunk, (below, above), passed in zip(CHUNKS, sent, passing):
        halo = (below, above, lax.ppermute(passed, both, onward))
        near, far, keep = pair_cross(flags, kinds, own, picks, flat, firsts, halo, chunk, token)
        near, far = (lax.ppermute(part, "day", swap(1)) for part in (near, far))
        if waiting is not None:
            lags = lag_sums(*waiting, lags, keep)
        pieces = pack(keep, near, far, keep if lags is None else lags, half)
        token = pieces[0]
        total = [pieces[0]] + [
            lax.ppermute(piece, "day", swap(2 * k)) for k, piece in enumerate(pieces) if k
        ]
        waiting = (lag_tables(width // 2, chunk, scale), sort, total)
    lags = lag_sums(*waiting, lags, None)
    return lags.T


def solution(mesh):
    placed = (P("tile", "day", None, None), P("tile"), P("tile"), P("tile"))
    return jax.shard_map(
        per_device, mesh=mesh, in_specs=placed, out_specs=P(("tile", "day"), None), check_vma=False
    )
```

time: 160 us -> 152 us (0.950)
  waiting for transfers between devices: 53.8 us -> 37.7 us
  starting transfers between devices: 29.4 us -> 38.6 us
  local copies, waits for them, and re-layouts: 8.9 us -> 6.06 us
    pallas_call x4 -> x6, Pallas kernels: 12.4 us -> 31.8 us  [the longest x1 16.5 us: own_cross(): pl.pallas_call(own_kernel, grid=(blocks, groups // SEG_STEP), in_specs=[s...]
    pallas_call x2, Pallas kernels: 41.8 us -> 24.1 us  [pair_cross(): pl.pallas_call(cross_kernel, grid=(parts, groups // SEG_STEP), in_specs=[...]
    ppermute x2, waiting for transfers between devices: 27.1 us -> 11.4 us  [per_device(): lax.ppermute(to_above, both, upward)]
    ppermute x4 -> x6, starting transfers between devices: 7.91 us -> 17.2 us  [the longest x4 14.5 us: per_device(): near, far = (lax.ppermute(part, 'day', swap(1)) for part in (near, far))]
    reshape x2 -> x0, local copies, waits for them, and re-layouts: 2.08 us -> none  [the longest x1 1.05 us: per_device(): second_ids = pair_second.reshape(members, kept)[order].reshape(pairs, 1)]
    ppermute x6, waiting for transfers between devices: 15.4 us -> 13.7 us  [per_device(): lax.ppermute(piece, 'day', swap(2 * k))]
    ppermute x4 -> x6, waiting for transfers between devices: 8.59 us -> 10 us  [the longest x2 7.62 us: per_device(): halo = (below, above, lax.ppermute(passed, both, onward))]
    unnamed x32 -> x28, local copies, waits for them, and re-layouts: 4.2 us -> 4.67 us
  transfers between devices with their start and end apart: 14 -> 16, of which waited for: 8 -> 11; matrix products, arithmetic and copies ran while one was open for 3% -> 1% of each run, Pallas kernels for 22% -> 36%
where the time goes in v2:
time: 152 us
  Pallas kernels  66.1 us (43%)
  starting transfers between devices  38.6 us (25%)
  waiting for transfers between devices  37.7 us (25%)
  local copies, waits for them, and re-layouts  6.06 us (4%)
  other arithmetic  1.89 us (1%)
    pallas_call x2, Pallas kernels, pair_cross(): pl.pallas_call(cross_kernel, grid=(parts, groups // SEG_STEP), in_specs=[...  24.1 us
    pallas_call x1, Pallas kernels, own_cross(): pl.pallas_call(own_kernel, grid=(blocks, groups // SEG_STEP), in_specs=[s...  16.5 us
    ppermute x4, starting transfers between devices, per_device(): near, far = (lax.ppermute(part, 'day', swap(1)) for part in (near, far))  14.5 us
    ppermute x6, waiting for transfers between devices, per_device(): lax.ppermute(piece, 'day', swap(2 * k))  13.7 us
    ppermute x2, starting transfers between devices, per_device(): lax.ppermute(to_above, both, upward)  12.4 us
    ppermute x2, waiting for transfers between devices, per_device(): lax.ppermute(to_above, both, upward)  11.4 us
    pallas_call x2, Pallas kernels, lent_rows(): pl.pallas_call(border_kernel, grid=(blocks, groups // step), in_specs=[sc...  10.2 us
    pallas_call x2, Pallas kernels, lag_sums(): pl.pallas_call(functools.partial(lag_kernel, len(total), int(base is not...  7.73 us
  transfers between devices with their start and end apart: 16, of which 11 were waited for; matrix products, arithmetic and copies ran while one was open for 1% of the time, Pallas kernels for 36%

profile of v2, /device:TPU:95, one launch (start us, length us, event | category | flops | bytes accessed | tf_op | source)
XLA Modules:
  0.0 151.8 jit_solution(11727557789858999451)
XLA Ops:
  0.0 1.4 copy.9.send_ref
  1.4 0.6 pad_add_fusion.flag_ref
  2.0 5.1 %shard_map.82 = (bf16[18,64,512]{2,1,0:T(8,128)(2,1)}, bf16[18,64,512]{2,1,0:T(8,128)(2,1)}, s32[2]{0:T(128)}) custom-call(s32[2]{0:T(128)} %pad_add_fusion.flag_ref, s32[128,1]{1,0:T(8,128)} %copy.9.send_ref, bf16[18,256,1024]{2,1,0:T(8,128)(2,1)} %bitcast.13, bf16[18,256,1024]{2,1,0:T(8,128)(2,1)} %bitcast.14), custom_call_target="tpu_custom_call" | custom-call | tf_op jit(solution)/shard_map/pallas_call | solution.py:66
  7.1 6.6 %collective-permute-start.3 = (bf16[18,64,512]{2,1,0:T(8,128)(2,1)}, bf16[18,64,512]{2,1,0:T(8,128)(2,1)S(1)}, u32[]{:S(2)}, u32[]{:S(2)}) collective-permute-start(bf16[18,64,512]{2,1,0:T(8,128)(2,1)} %get-tuple-element.45), channel_id=1, source_target_pairs={{120,0},{0,8},{8,16},{16,24},{24,32},{32,40},{40,48},{48,56},{56,6... | collective-permute-start | bytes 3538952 | tf_op jit(solution)/shard_map/ppermute | solution.py:435
  13.7 2.3 %collective-permute-start.4 = (bf16[18,64,512]{2,1,0:T(8,128)(2,1)}, bf16[18,64,512]{2,1,0:T(8,128)(2,1)}, u32[]{:S(2)}, u32[]{:S(2)}) collective-permute-start(bf16[18,64,512]{2,1,0:T(8,128)(2,1)} %get-tuple-element.46), channel_id=1, source_target_pairs={{128,120},{8,0},{16,8},{24,16},{32,24},{40,32},{48,40},{56,48},{64... | collective-permute-start | bytes 3538952 | tf_op jit(solution)/shard_map/ppermute | solution.py:435
  16.0 5.1 %shard_map.83 = (bf16[18,64,512]{2,1,0:T(8,128)(2,1)}, bf16[18,64,512]{2,1,0:T(8,128)(2,1)}, s32[2]{0:T(128)}) custom-call(s32[2]{0:T(128)} %get-tuple-element.33.flag_ref, s32[128,1]{1,0:T(8,128)} %copy.9.send_ref, bf16[18,256,1024]{2,1,0:T(8,128)(2,1)} %bitcast.15, bf16[18,256,1024]{2,1,0:T(8,128)(2,1)} %bitcast.16), custom_call_target="tpu_custom_call" | custom-call | tf_op jit(solution)/shard_map/pallas_call | solution.py:66
  21.1 5.8 %collective-permute-start = (bf16[18,64,512]{2,1,0:T(8,128)(2,1)}, bf16[18,64,512]{2,1,0:T(8,128)(2,1)S(1)}, u32[]{:S(2)}, u32[]{:S(2)}) collective-permute-start(bf16[18,64,512]{2,1,0:T(8,128)(2,1)} %get-tuple-element.42), channel_id=1, source_target_pairs={{120,0},{0,8},{8,16},{16,24},{24,32},{32,40},{40,48},{48,56},{56,6... | collective-permute-start | bytes 3538952 | tf_op jit(solution)/shard_map/ppermute | solution.py:435
  26.9 1.4 collective-permute-start.1
  28.3 2.5 %shard_map.84 = (bf16[4,512,256]{2,1,0:T(8,128)(2,1)}, bf16[4,256,128]{2,1,0:T(8,128)(2,1)}, bf16[128,128]{1,0:T(8,128)(2,1)}, s32[8]{0:T(128)}, s32[2]{0:T(128)}) custom-call(s32[2]{0:T(128)} %get-tuple-element.34.flag_ref, s32[8,128]{1,0:T(8,128)} %bitcast.24, s32[8,128]{1,0:T(8,128)} %bitcast.25), custom_call_target="tpu_custom_call" | custom-call | tf_op jit(solution)/shard_map/pallas_call | solution.py:138
  31.5 7.1 %collective-permute-done.3.below_ref = bf16[18,64,512]{2,1,0:T(8,128)(2,1)S(1)} collective-permute-done((bf16[18,64,512]{2,1,0:T(8,128)(2,1)}, bf16[18,64,512]{2,1,0:T(8,128)(2,1)S(1)}, u32[]{:S(2)}, u32[]{:S(2)}) %collective-permute-start.3) | collective-permute-done | bytes 1179680 | tf_op jit(solution)/shard_map/ppermute | solution.py:435
  38.6 1.3 collective-permute-done.4.above_ref
  39.9 1.2 broadcast_select_fusion
  41.1 1.3 collective-permute-start.5
  42.4 16.5 %shard_map.85 = (f32[512,1024]{1,0:T(8,128)}, f32[512,1024]{1,0:T(8,128)}, s32[2]{0:T(128)}) custom-call(s32[2]{0:T(128)} %get-tuple-element.36.flag_ref, s32[8]{0:T(128)} %get-tuple-element.37.kind_ref, bf16[4,512,256]{2,1,0:T(8,128)(2,1)} %get-tuple-element.38.own_ref, bf16[18,256,1024]{2,1,0:T(8,128)(2,1)} %bitcast.17, bf16[18,256,1024]{2,1,0:T(8,128)(2,1)} %bitcast.18), custom_call_target="tpu_custom_call" | custom-call | tf_op jit(solution)/shard_map/pallas_call | solution.py:208
  59.6 4.3 %collective-permute-done.below_ref = bf16[18,64,512]{2,1,0:T(8,128)(2,1)S(1)} collective-permute-done((bf16[18,64,512]{2,1,0:T(8,128)(2,1)}, bf16[18,64,512]{2,1,0:T(8,128)(2,1)S(1)}, u32[]{:S(2)}, u32[]{:S(2)}) %collective-permute-start) | collective-permute-done | bytes 1179680 | tf_op jit(solution)/shard_map/ppermute | solution.py:435
  63.9 1.3 collective-permute-done.1.above_ref
  65.2 0.1 broadcast_select_fusion.1.token_ref
  65.3 0.9 copy-done.1
  66.2 1.5 collective-permute-start.2
  67.7 5.8 %collective-permute-done.5.relay_ref = bf16[18,64,512]{2,1,0:T(8,128)(2,1)} collective-permute-done((bf16[18,64,512]{2,1,0:T(8,128)(2,1)}, bf16[18,64,512]{2,1,0:T(8,128)(2,1)}, u32[]{:S(2)}, u32[]{:S(2)}) %collective-permute-start.5) | collective-permute-done | bytes 1179680 | tf_op jit(solution)/shard_map/ppermute | solution.py:452
  73.5 12.0 %shard_map.86 = (f32[256,512]{1,0:T(8,128)}, f32[256,512]{1,0:T(8,128)}, f32[512,512]{1,0:T(8,128)}) custom-call(s32[2]{0:T(128)} %get-tuple-element.36.flag_ref, s32[8]{0:T(128)} %get-tuple-element.37.kind_ref, bf16[4,512,256]{2,1,0:T(8,128)(2,1)} %get-tuple-element.38.own_ref, bf16[4,256,128]{2,1,0:T(8,128)(2,1)} %get-tuple-element.39.halo_ref, ...), custom_call_target="tpu_custom_call" | custom-call | tf_op jit(solution)/shard_map/pallas_call | solution.py:285
  85.5 4.9 %collective-permute-start.6 = (f32[256,512]{1,0:T(8,128)}, f32[256,512]{1,0:T(8,128)S(1)}, u32[]{:S(2)}, u32[]{:S(2)}) collective-permute-start(f32[256,512]{1,0:T(8,128)} %get-tuple-element.48), channel_id=1, source_target_pairs={{0,1},{1,0},{2,3},{3,2},{4,5},{5,4},{6,7},{7,6},{8,9},{9,8},{10,11... | collective-permute-start | bytes 1572872 | tf_op jit(solution)/shard_map/ppermute | solution.py:454
  90.4 0.1 collective-permute-start.7
  90.5 1.6 %collective-permute-done.6.near_ref = f32[256,512]{1,0:T(8,128)S(1)} collective-permute-done((f32[256,512]{1,0:T(8,128)}, f32[256,512]{1,0:T(8,128)S(1)}, u32[]{:S(2)}, u32[]{:S(2)}) %collective-permute-start.6) | collective-permute-done | bytes 524320 | tf_op jit(solution)/shard_map/ppermute | solution.py:454
  92.2 0.7 collective-permute-done.7.far_ref
  92.9 0.0 copy-done.6
  92.9 0.8 copy-done.7
  93.7 2.5 %shard_map.87 = (f32[128,512]{1,0:T(8,128)}, s16[144,512]{1,0:T(8,128)(2,1)}, s16[144,512]{1,0:T(8,128)(2,1)}, s16[144,512]{1,0:T(8,128)(2,1)}) custom-call(f32[512,512]{1,0:T(8,128)} %get-tuple-element.47.keep_ref.token_ref, f32[256,512]{1,0:T(8,128)} %copy-done.6, f32[256,512]{1,0:T(8,128)} %copy-done.7, f32[512,512]{1,0:T(8,128)} %get-tuple-element.47.keep_ref.token_ref), custom_call_target="tpu_custom_call" | custom-call | flops 1 | bytes 1 | tf_op jit(solution)/shard_map/pallas_call | solution.py:330
  96.2 0.7 collective-permute-start.10
  96.9 0.0 collective-permute-start.11
  96.9 1.9 %collective-permute-start.12 = (s16[144,512]{1,0:T(8,128)(2,1)}, s16[144,512]{1,0:T(8,128)(2,1)S(1)}, u32[]{:S(2)}, u32[]{:S(2)}) collective-permute-start(s16[144,512]{1,0:T(8,128)(2,1)} %get-tuple-element.56), channel_id=1, source_target_pairs={{0,6},{1,7},{2,4},{3,5},{4,2},{5,3},{6,0},{7,1},{8,14},{9,15},{10,... | collective-permute-start | bytes 442376 | tf_op jit(solution)/shard_map/ppermute | solution.py:460
  98.9 1.8 %collective-permute-done.2.relay_ref = bf16[18,64,512]{2,1,0:T(8,128)(2,1)} collective-permute-done((bf16[18,64,512]{2,1,0:T(8,128)(2,1)S(1)}, bf16[18,64,512]{2,1,0:T(8,128)(2,1)}, u32[]{:S(2)}, u32[]{:S(2)}) %collective-permute-start.2) | collective-permute-done | bytes 1179680 | tf_op jit(solution)/shard_map/ppermute | solution.py:452
  100.7 12.1 %shard_map.88 = (f32[256,512]{1,0:T(8,128)}, f32[256,512]{1,0:T(8,128)}, f32[512,512]{1,0:T(8,128)}) custom-call(s32[2]{0:T(128)} %get-tuple-element.36.flag_ref, s32[8]{0:T(128)} %get-tuple-element.37.kind_ref, bf16[4,512,256]{2,1,0:T(8,128)(2,1)} %get-tuple-element.38.own_ref, bf16[4,256,128]{2,1,0:T(8,128)(2,1)} %get-tuple-element.39.halo_ref, ...), custom_call_target="tpu_custom_call" | custom-call | tf_op jit(solution)/shard_map/pallas_call | solution.py:285
  112.8 9.3 %collective-permute-start.8 = (f32[256,512]{1,0:T(8,128)}, f32[256,512]{1,0:T(8,128)S(1)}, u32[]{:S(2)}, u32[]{:S(2)}) collective-permute-start(f32[256,512]{1,0:T(8,128)} %get-tuple-element.52), channel_id=1, source_target_pairs={{0,1},{1,0},{2,3},{3,2},{4,5},{5,4},{6,7},{7,6},{8,9},{9,8},{10,11... | collective-permute-start | bytes 1572872 | tf_op jit(solution)/shard_map/ppermute | solution.py:454
  122.1 0.1 collective-permute-start.9
  122.2 0.6 copy-done.8
  122.9 0.0 copy-done.9
  122.9 0.1 copy-done.10
  123.0 3.8 %shard_map.89.token_ref.refs_4_ = f32[1001,128]{1,0:T(8,128)} custom-call(bf16[1001,512]{1,0:T(8,128)(2,1)} %constant.36.clone.coarse_ref, bf16[1001,512]{1,0:T(8,128)(2,1)} %constant.37.clone.fine_ref, bf16[128,128]{1,0:T(8,128)(2,1)} %get-tuple-element.35.sort_ref, f32[128,512]{1,0:T(8,128)} %get-tuple-element.50.token_ref.refs_0_, ...), custom_call_target="tpu_custom_call" | custom-call | flops 99999997952 | bytes 1000000000 | tf_op jit(solution)/shard_map/pallas_call | solution.py:373
  126.7 0.8 copy-done.4
  127.5 0.8 copy-done.5
  128.3 2.5 %shard_map.90 = (f32[128,512]{1,0:T(8,128)}, s16[144,512]{1,0:T(8,128)(2,1)}, s16[144,512]{1,0:T(8,128)(2,1)}, s16[144,512]{1,0:T(8,128)(2,1)}) custom-call(f32[512,512]{1,0:T(8,128)} %get-tuple-element.51.refs_4_.keep_ref, f32[256,512]{1,0:T(8,128)} %copy-done.4, f32[256,512]{1,0:T(8,128)} %copy-done.5, f32[1001,128]{1,0:T(8,128)} %shard_map.89.token_ref.refs_4_), custom_call_target="tpu_custom_call" | custom-call | flops 1 | bytes 1 | tf_op jit(solution)/shard_map/pallas_call | solution.py:330
  130.8 2.6 %collective-permute-start.15 = (s16[144,512]{1,0:T(8,128)(2,1)}, s16[144,512]{1,0:T(8,128)(2,1)S(1)}, u32[]{:S(2)}, u32[]{:S(2)}) collective-permute-start(s16[144,512]{1,0:T(8,128)(2,1)} %get-tuple-element.60), channel_id=1, source_target_pairs={{0,6},{1,7},{2,4},{3,5},{4,2},{5,3},{6,0},{7,1},{8,14},{9,15},{10,... | collective-permute-start | bytes 442376 | tf_op jit(solution)/shard_map/ppermute | solution.py:460
  133.5 2.6 %collective-permute-done.13.refs_1_ = s16[144,512]{1,0:T(8,128)(2,1)S(1)} collective-permute-done((s16[144,512]{1,0:T(8,128)(2,1)}, s16[144,512]{1,0:T(8,128)(2,1)S(1)}, u32[]{:S(2)}, u32[]{:S(2)}) %collective-permute-start.13) | collective-permute-done | bytes 147488 | tf_op jit(solution)/shard_map/ppermute | solution.py:460
  136.0 0.9 collective-permute-done.14.refs_2_
  137.0 10.2 %collective-permute-done.15.refs_3_ = s16[144,512]{1,0:T(8,128)(2,1)S(1)} collective-permute-done((s16[144,512]{1,0:T(8,128)(2,1)}, s16[144,512]{1,0:T(8,128)(2,1)S(1)}, u32[]{:S(2)}, u32[]{:S(2)}) %collective-permute-start.15) | collective-permute-done | bytes 147488 | tf_op jit(solution)/shard_map/ppermute | solution.py:460
  147.2 0.7 copy-done.13
  147.8 4.0 %shard_map.91 = f32[1001,128]{1,0:T(8,128)} custom-call(bf16[1001,512]{1,0:T(8,128)(2,1)} %constant.38.clone.coarse_ref, bf16[1001,512]{1,0:T(8,128)(2,1)} %constant.39.clone.fine_ref, bf16[128,128]{1,0:T(8,128)(2,1)} %get-tuple-element.35.sort_ref, f32[128,512]{1,0:T(8,128)} %get-tuple-element.57.refs_0_, s16[144,512]{1,0:T(8,128)(2,1)} %copy-done.11, ...), custom_call_target="tpu_custom_call" | custom-call | flops 99999997952 | bytes 1000000000 | tf_op jit(solution)/shard_map/pallas_call | solution.py:373
  (26 shorter events, 0.1 us)
Async XLA Ops:
  7.1 31.5 %collective-permute-start.3 = (bf16[18,64,512]{2,1,0:T(8,128)(2,1)}, bf16[18,64,512]{2,1,0:T(8,128)(2,1)S(1)}, u32[]{:S(2)}, u32[]{:S(2)}) collective-permute-start(bf16[18,64,512]{2,1,0:T(8,128)(2,1)} %get-tuple-element.45), channel_id=1, source_target_pairs={{120,0},{0,8},{8,16},{16,24},{24,32},{32,40},{40,48},{48,56},{56,6... | collective-permute-start | bytes 3538952 | tf_op jit(solution)/shard_map/ppermute | solution.py:435
  13.7 26.2 %collective-permute-start.4 = (bf16[18,64,512]{2,1,0:T(8,128)(2,1)}, bf16[18,64,512]{2,1,0:T(8,128)(2,1)}, u32[]{:S(2)}, u32[]{:S(2)}) collective-permute-start(bf16[18,64,512]{2,1,0:T(8,128)(2,1)} %get-tuple-element.46), channel_id=1, source_target_pairs={{128,120},{8,0},{16,8},{24,16},{32,24},{40,32},{48,40},{56,48},{64... | collective-permute-start | bytes 3538952 | tf_op jit(solution)/shard_map/ppermute | solution.py:435
  21.1 42.8 %collective-permute-start = (bf16[18,64,512]{2,1,0:T(8,128)(2,1)}, bf16[18,64,512]{2,1,0:T(8,128)(2,1)S(1)}, u32[]{:S(2)}, u32[]{:S(2)}) collective-permute-start(bf16[18,64,512]{2,1,0:T(8,128)(2,1)} %get-tuple-element.42), channel_id=1, source_target_pairs={{120,0},{0,8},{8,16},{16,24},{24,32},{32,40},{40,48},{48,56},{56,6... | collective-permute-start | bytes 3538952 | tf_op jit(solution)/shard_map/ppermute | solution.py:435
  26.9 38.2 %collective-permute-start.1 = (bf16[18,64,512]{2,1,0:T(8,128)(2,1)}, bf16[18,64,512]{2,1,0:T(8,128)(2,1)S(1)}, u32[]{:S(2)}, u32[]{:S(2)}) collective-permute-start(bf16[18,64,512]{2,1,0:T(8,128)(2,1)} %get-tuple-element.43), channel_id=1, source_target_pairs={{128,120},{8,0},{16,8},{24,16},{32,24},{40,32},{48,40},{56,48},{64... | collective-permute-start | bytes 3538952 | tf_op jit(solution)/shard_map/ppermute | solution.py:435
  38.6 2.5 %copy-start.2 = (bf16[18,64,512]{2,1,0:T(8,128)(2,1)}, bf16[18,64,512]{2,1,0:T(8,128)(2,1)S(1)}, u32[]{:S(2)}) copy-start(bf16[18,64,512]{2,1,0:T(8,128)(2,1)S(1)} %collective-permute-done.3.below_ref) | copy-start | bytes 3538948
  41.1 32.4 %collective-permute-start.5 = (bf16[18,64,512]{2,1,0:T(8,128)(2,1)}, bf16[18,64,512]{2,1,0:T(8,128)(2,1)}, u32[]{:S(2)}, u32[]{:S(2)}) collective-permute-start(bf16[18,64,512]{2,1,0:T(8,128)(2,1)} %broadcast_select_fusion), channel_id=1, source_target_pairs={{0,128},{1,129},{2,130},{3,131},{252,124},{253,125},{254,126},{255... | collective-permute-start | bytes 3538952 | tf_op jit(solution)/shard_map/ppermute | solution.py:452
  63.9 1.4 copy-start
  65.2 1.0 copy-start.1
  66.2 7.3 %copy-start.3 = (bf16[18,64,512]{2,1,0:T(8,128)(2,1)}, bf16[18,64,512]{2,1,0:T(8,128)(2,1)S(1)}, u32[]{:S(2)}) copy-start(bf16[18,64,512]{2,1,0:T(8,128)(2,1)S(1)} %broadcast_select_fusion.1.token_ref) | copy-start | bytes 3538948
  66.2 34.5 %collective-permute-start.2 = (bf16[18,64,512]{2,1,0:T(8,128)(2,1)S(1)}, bf16[18,64,512]{2,1,0:T(8,128)(2,1)}, u32[]{:S(2)}, u32[]{:S(2)}) collective-permute-start(bf16[18,64,512]{2,1,0:T(8,128)(2,1)S(1)} %broadcast_select_fusion.1.token_ref), channel_id=1, source_target_pairs={{0,128},{1,129},{2,130},{3,131},{252,124},{253,125},{254,126},{255... | collective-permute-start | bytes 3538952 | tf_op jit(solution)/shard_map/ppermute | solution.py:452
  85.5 6.7 %collective-permute-start.6 = (f32[256,512]{1,0:T(8,128)}, f32[256,512]{1,0:T(8,128)S(1)}, u32[]{:S(2)}, u32[]{:S(2)}) collective-permute-start(f32[256,512]{1,0:T(8,128)} %get-tuple-element.48), channel_id=1, source_target_pairs={{0,1},{1,0},{2,3},{3,2},{4,5},{5,4},{6,7},{7,6},{8,9},{9,8},{10,11... | collective-permute-start | bytes 1572872 | tf_op jit(solution)/shard_map/ppermute | solution.py:454
  90.4 2.5 %collective-permute-start.7 = (f32[256,512]{1,0:T(8,128)}, f32[256,512]{1,0:T(8,128)S(1)}, u32[]{:S(2)}, u32[]{:S(2)}) collective-permute-start(f32[256,512]{1,0:T(8,128)} %get-tuple-element.49), channel_id=1, source_target_pairs={{0,1},{1,0},{2,3},{3,2},{4,5},{5,4},{6,7},{7,6},{8,9},{9,8},{10,11... | collective-permute-start | bytes 1572872 | tf_op jit(solution)/shard_map/ppermute | solution.py:454
  92.2 0.8 copy-start.6
  92.9 0.8 copy-start.7
  96.2 26.0 %collective-permute-start.10 = (s16[144,512]{1,0:T(8,128)(2,1)}, s16[144,512]{1,0:T(8,128)(2,1)S(1)}, u32[]{:S(2)}, u32[]{:S(2)}) collective-permute-start(s16[144,512]{1,0:T(8,128)(2,1)} %get-tuple-element.54), channel_id=1, source_target_pairs={{0,2},{1,3},{2,0},{3,1},{4,6},{5,7},{6,4},{7,5},{8,10},{9,11},{10,... | collective-permute-start | bytes 442376 | tf_op jit(solution)/shard_map/ppermute | solution.py:460
  96.9 25.3 %collective-permute-start.11 = (s16[144,512]{1,0:T(8,128)(2,1)}, s16[144,512]{1,0:T(8,128)(2,1)S(1)}, u32[]{:S(2)}, u32[]{:S(2)}) collective-permute-start(s16[144,512]{1,0:T(8,128)(2,1)} %get-tuple-element.55), channel_id=1, source_target_pairs={{0,4},{1,5},{2,6},{3,7},{4,0},{5,1},{6,2},{7,3},{8,12},{9,13},{10,... | collective-permute-start | bytes 442376 | tf_op jit(solution)/shard_map/ppermute | solution.py:460
  96.9 25.3 %collective-permute-start.12 = (s16[144,512]{1,0:T(8,128)(2,1)}, s16[144,512]{1,0:T(8,128)(2,1)S(1)}, u32[]{:S(2)}, u32[]{:S(2)}) collective-permute-start(s16[144,512]{1,0:T(8,128)(2,1)} %get-tuple-element.56), channel_id=1, source_target_pairs={{0,6},{1,7},{2,4},{3,5},{4,2},{5,3},{6,0},{7,1},{8,14},{9,15},{10,... | collective-permute-start | bytes 442376 | tf_op jit(solution)/shard_map/ppermute | solution.py:460
  112.8 14.0 %collective-permute-start.8 = (f32[256,512]{1,0:T(8,128)}, f32[256,512]{1,0:T(8,128)S(1)}, u32[]{:S(2)}, u32[]{:S(2)}) collective-permute-start(f32[256,512]{1,0:T(8,128)} %get-tuple-element.52), channel_id=1, source_target_pairs={{0,1},{1,0},{2,3},{3,2},{4,5},{5,4},{6,7},{7,6},{8,9},{9,8},{10,11... | collective-permute-start | bytes 1572872 | tf_op jit(solution)/shard_map/ppermute | solution.py:454
  122.1 4.7 %collective-permute-start.9 = (f32[256,512]{1,0:T(8,128)}, f32[256,512]{1,0:T(8,128)S(1)}, u32[]{:S(2)}, u32[]{:S(2)}) collective-permute-start(f32[256,512]{1,0:T(8,128)} %get-tuple-element.53), channel_id=1, source_target_pairs={{0,1},{1,0},{2,3},{3,2},{4,5},{5,4},{6,7},{7,6},{8,9},{9,8},{10,11... | collective-permute-start | bytes 1572872 | tf_op jit(solution)/shard_map/ppermute | solution.py:454
  122.2 0.7 copy-start.8
  122.2 0.7 copy-start.9
  122.2 0.7 copy-start.10
  126.7 0.8 copy-start.4
  127.5 0.8 copy-start.5
  130.8 5.2 %collective-permute-start.13 = (s16[144,512]{1,0:T(8,128)(2,1)}, s16[144,512]{1,0:T(8,128)(2,1)S(1)}, u32[]{:S(2)}, u32[]{:S(2)}) collective-permute-start(s16[144,512]{1,0:T(8,128)(2,1)} %get-tuple-element.58), channel_id=1, source_target_pairs={{0,2},{1,3},{2,0},{3,1},{4,6},{5,7},{6,4},{7,5},{8,10},{9,11},{10,... | collective-permute-start | bytes 442376 | tf_op jit(solution)/shard_map/ppermute | solution.py:460
  130.8 6.2 %collective-permute-start.14 = (s16[144,512]{1,0:T(8,128)(2,1)}, s16[144,512]{1,0:T(8,128)(2,1)S(1)}, u32[]{:S(2)}, u32[]{:S(2)}) collective-permute-start(s16[144,512]{1,0:T(8,128)(2,1)} %get-tuple-element.59), channel_id=1, source_target_pairs={{0,4},{1,5},{2,6},{3,7},{4,0},{5,1},{6,2},{7,3},{8,12},{9,13},{10,... | collective-permute-start | bytes 442376 | tf_op jit(solution)/shard_map/ppermute | solution.py:460
  130.8 16.4 %collective-permute-start.15 = (s16[144,512]{1,0:T(8,128)(2,1)}, s16[144,512]{1,0:T(8,128)(2,1)S(1)}, u32[]{:S(2)}, u32[]{:S(2)}) collective-permute-start(s16[144,512]{1,0:T(8,128)(2,1)} %get-tuple-element.60), channel_id=1, source_target_pairs={{0,6},{1,7},{2,4},{3,5},{4,2},{5,3},{6,0},{7,1},{8,14},{9,15},{10,... | collective-permute-start | bytes 442376 | tf_op jit(solution)/shard_map/ppermute | solution.py:460
  136.0 11.1 %copy-start.11 = (s16[144,512]{1,0:T(8,128)(2,1)}, s16[144,512]{1,0:T(8,128)(2,1)S(1)}, u32[]{:S(2)}) copy-start(s16[144,512]{1,0:T(8,128)(2,1)S(1)} %collective-permute-done.13.refs_1_) | copy-start | bytes 442372
  137.0 10.2 %copy-start.12 = (s16[144,512]{1,0:T(8,128)(2,1)}, s16[144,512]{1,0:T(8,128)(2,1)S(1)}, u32[]{:S(2)}) copy-start(s16[144,512]{1,0:T(8,128)(2,1)S(1)} %collective-permute-done.14.refs_2_) | copy-start | bytes 442372
  147.2 0.7 copy-start.13

commit v3 on v2

--- a/solution.py
+++ b/solution.py
@@ -18,11 +18,6 @@
 TOP = 32000.0
 
 
-def one_hot(ids, width, base):
-    slots = lax.broadcasted_iota(jnp.int32, (ids.shape[0], width), 1) + base
-    return (ids == slots).astype(jnp.float32).astype(jnp.bfloat16)
-
-
 def anywhere():
     return pl.BlockSpec(memory_space=pl.ANY)
 
@@ -41,7 +36,15 @@
 
     @pl.when((pl.program_id(0) == 0) & (pl.program_id(1) == 0))
     def _():
-        pick_ref[...] = one_hot(send_ref[...], pick_ref.shape[1], 0)
+        count, stations = pick_ref.shape
+        slots = lax.broadcasted_iota(jnp.int32, (stations, count), 0)
+        columns = (send_ref[...] == slots).astype(jnp.float32).astype(jnp.bfloat16)
+        down = lax.broadcasted_iota(jnp.int32, (count, count), 0)
+        across = lax.broadcasted_iota(jnp.int32, (count, count), 1)
+        same = (down == across).astype(jnp.float32).astype(jnp.bfloat16)
+        dims = (((1,), (1,)), ((), ()))
+        turned = lax.dot_general(same, columns, dims, preferred_element_type=jnp.float32)
+        pick_ref[...] = turned.astype(jnp.bfloat16)
 
     half = below_ref.shape[1]
     step = real_ref.shape[0]
@@ -68,7 +71,7 @@
         grid=(blocks, groups // step),
         in_specs=[
             scalars(),
-            pl.BlockSpec((count, 1), lambda j, g: (0, 0)),
+            pl.BlockSpec((1, count), lambda j, g: (0, 0)),
             pl.BlockSpec((step, stations, LANES), lambda j, g: (g, 0, first + j)),
             pl.BlockSpec((step, stations, LANES), lambda j, g: (g, 0, first + j + offset)),
         ],
@@ -76,7 +79,7 @@
         out_shape=[out, out, jax.ShapeDtypeStruct((2,), jnp.int32)],
         scratch_shapes=[pltpu.VMEM((count, stations), jnp.bfloat16)],
         compiler_params=params(),
-    )(flags, send_list.reshape(count, 1), spectra, spectra)
+    )(flags, send_list.reshape(1, count), spectra, spectra)
 
 
 def prepare_kernel(

time: 152 us -> 151 us (level)
  no operation moved by 1% of the time
where the time goes in v3:
time: 151 us
  Pallas kernels  66.3 us (44%)
  starting transfers between devices  38.5 us (25%)
  waiting for transfers between devices  37.7 us (25%)
  local copies, waits for them, and re-layouts  4.74 us (3%)
  other arithmetic  1.97 us (1%)
    pallas_call x2, Pallas kernels, pair_cross(): pl.pallas_call(cross_kernel, grid=(parts, groups // SEG_STEP), in_specs=[...  24.1 us
    pallas_call x1, Pallas kernels, own_cross(): pl.pallas_call(own_kernel, grid=(blocks, groups // SEG_STEP), in_specs=[s...  16.5 us
    ppermute x4, starting transfers between devices, per_device(): near, far = (lax.ppermute(part, 'day', swap(1)) for part in (near, far))  14.3 us
    ppermute x6, waiting for transfers between devices, per_device(): lax.ppermute(piece, 'day', swap(2 * k))  13.7 us
    ppermute x2, starting transfers between devices, per_device(): lax.ppermute(to_above, both, upward)  12.4 us
    ppermute x2, waiting for transfers between devices, per_device(): lax.ppermute(to_above, both, upward)  11.3 us
    pallas_call x2, Pallas kernels, lent_rows(): pl.pallas_call(border_kernel, grid=(blocks, groups // step), in_specs=[sc...  10.4 us
    pallas_call x2, Pallas kernels, lag_sums(): pl.pallas_call(functools.partial(lag_kernel, len(total), int(base is not...  7.79 us
  transfers between devices with their start and end apart: 16, of which 11 were waited for; matrix products, arithmetic and copies ran while one was open for 1% of the time, Pallas kernels for 36%

profile of v3, /device:TPU:95, one launch (start us, length us, event | category | flops | bytes accessed | tf_op | source)
XLA Modules:
  0.0 150.6 jit_solution(13895747155582879430)
XLA Ops:
  0.0 0.7 pad_add_fusion.flag_ref
  0.7 5.2 %shard_map.82 = (bf16[18,64,512]{2,1,0:T(8,128)(2,1)}, bf16[18,64,512]{2,1,0:T(8,128)(2,1)}, s32[2]{0:T(128)}) custom-call(s32[2]{0:T(128)} %pad_add_fusion.flag_ref, s32[1,128]{1,0:T(1,128)} %bitcast.26, bf16[18,256,1024]{2,1,0:T(8,128)(2,1)} %bitcast.13, bf16[18,256,1024]{2,1,0:T(8,128)(2,1)} %bitcast.14), custom_call_target="tpu_custom_call" | custom-call | tf_op jit(solution)/shard_map/pallas_call | solution.py:69
  5.9 6.6 %collective-permute-start.3 = (bf16[18,64,512]{2,1,0:T(8,128)(2,1)}, bf16[18,64,512]{2,1,0:T(8,128)(2,1)S(1)}, u32[]{:S(2)}, u32[]{:S(2)}) collective-permute-start(bf16[18,64,512]{2,1,0:T(8,128)(2,1)} %get-tuple-element.45), channel_id=1, source_target_pairs={{120,0},{0,8},{8,16},{16,24},{24,32},{32,40},{40,48},{48,56},{56,6... | collective-permute-start | bytes 3538952 | tf_op jit(solution)/shard_map/ppermute | solution.py:438
  12.4 2.3 %collective-permute-start.4 = (bf16[18,64,512]{2,1,0:T(8,128)(2,1)}, bf16[18,64,512]{2,1,0:T(8,128)(2,1)}, u32[]{:S(2)}, u32[]{:S(2)}) collective-permute-start(bf16[18,64,512]{2,1,0:T(8,128)(2,1)} %get-tuple-element.46), channel_id=1, source_target_pairs={{128,120},{8,0},{16,8},{24,16},{32,24},{40,32},{48,40},{56,48},{64... | collective-permute-start | bytes 3538952 | tf_op jit(solution)/shard_map/ppermute | solution.py:438
  14.8 5.2 %shard_map.83 = (bf16[18,64,512]{2,1,0:T(8,128)(2,1)}, bf16[18,64,512]{2,1,0:T(8,128)(2,1)}, s32[2]{0:T(128)}) custom-call(s32[2]{0:T(128)} %get-tuple-element.33.flag_ref, s32[1,128]{1,0:T(1,128)} %bitcast.27, bf16[18,256,1024]{2,1,0:T(8,128)(2,1)} %bitcast.15, bf16[18,256,1024]{2,1,0:T(8,128)(2,1)} %bitcast.16), custom_call_target="tpu_custom_call" | custom-call | tf_op jit(solution)/shard_map/pallas_call | solution.py:69
  19.9 5.8 %collective-permute-start = (bf16[18,64,512]{2,1,0:T(8,128)(2,1)}, bf16[18,64,512]{2,1,0:T(8,128)(2,1)S(1)}, u32[]{:S(2)}, u32[]{:S(2)}) collective-permute-start(bf16[18,64,512]{2,1,0:T(8,128)(2,1)} %get-tuple-element.42), channel_id=1, source_target_pairs={{120,0},{0,8},{8,16},{16,24},{24,32},{32,40},{40,48},{48,56},{56,6... | collective-permute-start | bytes 3538952 | tf_op jit(solution)/shard_map/ppermute | solution.py:438
  25.8 1.4 collective-permute-start.1
  27.2 2.5 %shard_map.84 = (bf16[4,512,256]{2,1,0:T(8,128)(2,1)}, bf16[4,256,128]{2,1,0:T(8,128)(2,1)}, bf16[128,128]{1,0:T(8,128)(2,1)}, s32[8]{0:T(128)}, s32[2]{0:T(128)}) custom-call(s32[2]{0:T(128)} %get-tuple-element.34.flag_ref, s32[8,128]{1,0:T(8,128)} %bitcast.24, s32[8,128]{1,0:T(8,128)} %bitcast.25), custom_call_target="tpu_custom_call" | custom-call | tf_op jit(solution)/shard_map/pallas_call | solution.py:141
  30.3 7.1 %collective-permute-done.3.below_ref = bf16[18,64,512]{2,1,0:T(8,128)(2,1)S(1)} collective-permute-done((bf16[18,64,512]{2,1,0:T(8,128)(2,1)}, bf16[18,64,512]{2,1,0:T(8,128)(2,1)S(1)}, u32[]{:S(2)}, u32[]{:S(2)}) %collective-permute-start.3) | collective-permute-done | bytes 1179680 | tf_op jit(solution)/shard_map/ppermute | solution.py:438
  37.4 1.3 collective-permute-done.4.above_ref
  38.7 1.2 broadcast_select_fusion
  39.9 1.3 collective-permute-start.5
  41.1 16.5 %shard_map.85 = (f32[512,1024]{1,0:T(8,128)}, f32[512,1024]{1,0:T(8,128)}, s32[2]{0:T(128)}) custom-call(s32[2]{0:T(128)} %get-tuple-element.36.flag_ref, s32[8]{0:T(128)} %get-tuple-element.37.kind_ref, bf16[4,512,256]{2,1,0:T(8,128)(2,1)} %get-tuple-element.38.own_ref, bf16[18,256,1024]{2,1,0:T(8,128)(2,1)} %bitcast.17, bf16[18,256,1024]{2,1,0:T(8,128)(2,1)} %bitcast.18), custom_call_target="tpu_custom_call" | custom-call | tf_op jit(solution)/shard_map/pallas_call | solution.py:211
  58.4 4.3 %collective-permute-done.below_ref = bf16[18,64,512]{2,1,0:T(8,128)(2,1)S(1)} collective-permute-done((bf16[18,64,512]{2,1,0:T(8,128)(2,1)}, bf16[18,64,512]{2,1,0:T(8,128)(2,1)S(1)}, u32[]{:S(2)}, u32[]{:S(2)}) %collective-permute-start) | collective-permute-done | bytes 1179680 | tf_op jit(solution)/shard_map/ppermute | solution.py:438
  62.7 1.3 collective-permute-done.1.above_ref
  64.0 0.1 broadcast_select_fusion.1.token_ref
  64.1 0.9 copy-done.1
  65.0 1.5 collective-permute-start.2
  66.5 5.7 %collective-permute-done.5.relay_ref = bf16[18,64,512]{2,1,0:T(8,128)(2,1)} collective-permute-done((bf16[18,64,512]{2,1,0:T(8,128)(2,1)}, bf16[18,64,512]{2,1,0:T(8,128)(2,1)}, u32[]{:S(2)}, u32[]{:S(2)}) %collective-permute-start.5) | collective-permute-done | bytes 1179680 | tf_op jit(solution)/shard_map/ppermute | solution.py:455
  72.2 12.0 %shard_map.86 = (f32[256,512]{1,0:T(8,128)}, f32[256,512]{1,0:T(8,128)}, f32[512,512]{1,0:T(8,128)}) custom-call(s32[2]{0:T(128)} %get-tuple-element.36.flag_ref, s32[8]{0:T(128)} %get-tuple-element.37.kind_ref, bf16[4,512,256]{2,1,0:T(8,128)(2,1)} %get-tuple-element.38.own_ref, bf16[4,256,128]{2,1,0:T(8,128)(2,1)} %get-tuple-element.39.halo_ref, ...), custom_call_target="tpu_custom_call" | custom-call | tf_op jit(solution)/shard_map/pallas_call | solution.py:288
  84.2 4.9 %collective-permute-start.6 = (f32[256,512]{1,0:T(8,128)}, f32[256,512]{1,0:T(8,128)S(1)}, u32[]{:S(2)}, u32[]{:S(2)}) collective-permute-start(f32[256,512]{1,0:T(8,128)} %get-tuple-element.48), channel_id=1, source_target_pairs={{0,1},{1,0},{2,3},{3,2},{4,5},{5,4},{6,7},{7,6},{8,9},{9,8},{10,11... | collective-permute-start | bytes 1572872 | tf_op jit(solution)/shard_map/ppermute | solution.py:457
  89.1 0.1 collective-permute-start.7
  89.2 1.6 %collective-permute-done.6.near_ref = f32[256,512]{1,0:T(8,128)S(1)} collective-permute-done((f32[256,512]{1,0:T(8,128)}, f32[256,512]{1,0:T(8,128)S(1)}, u32[]{:S(2)}, u32[]{:S(2)}) %collective-permute-start.6) | collective-permute-done | bytes 524320 | tf_op jit(solution)/shard_map/ppermute | solution.py:457
  90.9 0.7 collective-permute-done.7.far_ref
  91.6 0.0 copy-done.6
  91.7 0.8 copy-done.7
  92.4 2.5 %shard_map.87 = (f32[128,512]{1,0:T(8,128)}, s16[144,512]{1,0:T(8,128)(2,1)}, s16[144,512]{1,0:T(8,128)(2,1)}, s16[144,512]{1,0:T(8,128)(2,1)}) custom-call(f32[512,512]{1,0:T(8,128)} %get-tuple-element.47.keep_ref.token_ref, f32[256,512]{1,0:T(8,128)} %copy-done.6, f32[256,512]{1,0:T(8,128)} %copy-done.7, f32[512,512]{1,0:T(8,128)} %get-tuple-element.47.keep_ref.token_ref), custom_call_target="tpu_custom_call" | custom-call | flops 1 | bytes 1 | tf_op jit(solution)/shard_map/pallas_call | solution.py:333
  94.9 0.8 collective-permute-start.10
  95.7 1.9 %collective-permute-start.12 = (s16[144,512]{1,0:T(8,128)(2,1)}, s16[144,512]{1,0:T(8,128)(2,1)S(1)}, u32[]{:S(2)}, u32[]{:S(2)}) collective-permute-start(s16[144,512]{1,0:T(8,128)(2,1)} %get-tuple-element.56), channel_id=1, source_target_pairs={{0,6},{1,7},{2,4},{3,5},{4,2},{5,3},{6,0},{7,1},{8,14},{9,15},{10,... | collective-permute-start | bytes 442376 | tf_op jit(solution)/shard_map/ppermute | solution.py:463
  97.6 1.9 %collective-permute-done.2.relay_ref = bf16[18,64,512]{2,1,0:T(8,128)(2,1)} collective-permute-done((bf16[18,64,512]{2,1,0:T(8,128)(2,1)S(1)}, bf16[18,64,512]{2,1,0:T(8,128)(2,1)}, u32[]{:S(2)}, u32[]{:S(2)}) %collective-permute-start.2) | collective-permute-done | bytes 1179680 | tf_op jit(solution)/shard_map/ppermute | solution.py:455
  99.5 12.1 %shard_map.88 = (f32[256,512]{1,0:T(8,128)}, f32[256,512]{1,0:T(8,128)}, f32[512,512]{1,0:T(8,128)}) custom-call(s32[2]{0:T(128)} %get-tuple-element.36.flag_ref, s32[8]{0:T(128)} %get-tuple-element.37.kind_ref, bf16[4,512,256]{2,1,0:T(8,128)(2,1)} %get-tuple-element.38.own_ref, bf16[4,256,128]{2,1,0:T(8,128)(2,1)} %get-tuple-element.39.halo_ref, ...), custom_call_target="tpu_custom_call" | custom-call | tf_op jit(solution)/shard_map/pallas_call | solution.py:288
  111.6 9.2 %collective-permute-start.8 = (f32[256,512]{1,0:T(8,128)}, f32[256,512]{1,0:T(8,128)S(1)}, u32[]{:S(2)}, u32[]{:S(2)}) collective-permute-start(f32[256,512]{1,0:T(8,128)} %get-tuple-element.52), channel_id=1, source_target_pairs={{0,1},{1,0},{2,3},{3,2},{4,5},{5,4},{6,7},{7,6},{8,9},{9,8},{10,11... | collective-permute-start | bytes 1572872 | tf_op jit(solution)/shard_map/ppermute | solution.py:457
  120.8 0.1 collective-permute-start.9
  120.9 0.0 collective-permute-done.11.refs_2_
  120.9 0.0 collective-permute-done.12.refs_3_
  120.9 0.6 copy-done.8
  121.6 0.1 copy-done.9
  121.6 0.0 copy-done.10
  121.7 3.8 %shard_map.89.token_ref.refs_4_ = f32[1001,128]{1,0:T(8,128)} custom-call(bf16[1001,512]{1,0:T(8,128)(2,1)} %constant.36.clone.coarse_ref, bf16[1001,512]{1,0:T(8,128)(2,1)} %constant.37.clone.fine_ref, bf16[128,128]{1,0:T(8,128)(2,1)} %get-tuple-element.35.sort_ref, f32[128,512]{1,0:T(8,128)} %get-tuple-element.50.token_ref.refs_0_, ...), custom_call_target="tpu_custom_call" | custom-call | flops 99999997952 | bytes 1000000000 | tf_op jit(solution)/shard_map/pallas_call | solution.py:376
  125.5 0.8 copy-done.4
  126.4 0.8 copy-done.5
  127.1 2.5 %shard_map.90 = (f32[128,512]{1,0:T(8,128)}, s16[144,512]{1,0:T(8,128)(2,1)}, s16[144,512]{1,0:T(8,128)(2,1)}, s16[144,512]{1,0:T(8,128)(2,1)}) custom-call(f32[512,512]{1,0:T(8,128)} %get-tuple-element.51.refs_4_.keep_ref, f32[256,512]{1,0:T(8,128)} %copy-done.4, f32[256,512]{1,0:T(8,128)} %copy-done.5, f32[1001,128]{1,0:T(8,128)} %shard_map.89.token_ref.refs_4_), custom_call_target="tpu_custom_call" | custom-call | flops 1 | bytes 1 | tf_op jit(solution)/shard_map/pallas_call | solution.py:333
  129.7 2.6 %collective-permute-start.15 = (s16[144,512]{1,0:T(8,128)(2,1)}, s16[144,512]{1,0:T(8,128)(2,1)S(1)}, u32[]{:S(2)}, u32[]{:S(2)}) collective-permute-start(s16[144,512]{1,0:T(8,128)(2,1)} %get-tuple-element.60), channel_id=1, source_target_pairs={{0,6},{1,7},{2,4},{3,5},{4,2},{5,3},{6,0},{7,1},{8,14},{9,15},{10,... | collective-permute-start | bytes 442376 | tf_op jit(solution)/shard_map/ppermute | solution.py:463
  132.3 2.6 %collective-permute-done.13.refs_1_ = s16[144,512]{1,0:T(8,128)(2,1)S(1)} collective-permute-done((s16[144,512]{1,0:T(8,128)(2,1)}, s16[144,512]{1,0:T(8,128)(2,1)S(1)}, u32[]{:S(2)}, u32[]{:S(2)}) %collective-permute-start.13) | collective-permute-done | bytes 147488 | tf_op jit(solution)/shard_map/ppermute | solution.py:463
  134.9 0.9 collective-permute-done.14.refs_2_
  135.8 10.2 %collective-permute-done.15.refs_3_ = s16[144,512]{1,0:T(8,128)(2,1)S(1)} collective-permute-done((s16[144,512]{1,0:T(8,128)(2,1)}, s16[144,512]{1,0:T(8,128)(2,1)S(1)}, u32[]{:S(2)}, u32[]{:S(2)}) %collective-permute-start.15) | collective-permute-done | bytes 147488 | tf_op jit(solution)/shard_map/ppermute | solution.py:463
  146.0 0.7 copy-done.13
  146.7 4.0 %shard_map.91 = f32[1001,128]{1,0:T(8,128)} custom-call(bf16[1001,512]{1,0:T(8,128)(2,1)} %constant.38.clone.coarse_ref, bf16[1001,512]{1,0:T(8,128)(2,1)} %constant.39.clone.fine_ref, bf16[128,128]{1,0:T(8,128)(2,1)} %get-tuple-element.35.sort_ref, f32[128,512]{1,0:T(8,128)} %get-tuple-element.57.refs_0_, s16[144,512]{1,0:T(8,128)(2,1)} %copy-done.11, ...), custom_call_target="tpu_custom_call" | custom-call | flops 99999997952 | bytes 1000000000 | tf_op jit(solution)/shard_map/pallas_call | solution.py:376
  (25 shorter events, 0.0 us)
Async XLA Ops:
  5.9 31.5 %collective-permute-start.3 = (bf16[18,64,512]{2,1,0:T(8,128)(2,1)}, bf16[18,64,512]{2,1,0:T(8,128)(2,1)S(1)}, u32[]{:S(2)}, u32[]{:S(2)}) collective-permute-start(bf16[18,64,512]{2,1,0:T(8,128)(2,1)} %get-tuple-element.45), channel_id=1, source_target_pairs={{120,0},{0,8},{8,16},{16,24},{24,32},{32,40},{40,48},{48,56},{56,6... | collective-permute-start | bytes 3538952 | tf_op jit(solution)/shard_map/ppermute | solution.py:438
  12.4 26.2 %collective-permute-start.4 = (bf16[18,64,512]{2,1,0:T(8,128)(2,1)}, bf16[18,64,512]{2,1,0:T(8,128)(2,1)}, u32[]{:S(2)}, u32[]{:S(2)}) collective-permute-start(bf16[18,64,512]{2,1,0:T(8,128)(2,1)} %get-tuple-element.46), channel_id=1, source_target_pairs={{128,120},{8,0},{16,8},{24,16},{32,24},{40,32},{48,40},{56,48},{64... | collective-permute-start | bytes 3538952 | tf_op jit(solution)/shard_map/ppermute | solution.py:438
  19.9 42.7 %collective-permute-start = (bf16[18,64,512]{2,1,0:T(8,128)(2,1)}, bf16[18,64,512]{2,1,0:T(8,128)(2,1)S(1)}, u32[]{:S(2)}, u32[]{:S(2)}) collective-permute-start(bf16[18,64,512]{2,1,0:T(8,128)(2,1)} %get-tuple-element.42), channel_id=1, source_target_pairs={{120,0},{0,8},{8,16},{16,24},{24,32},{32,40},{40,48},{48,56},{56,6... | collective-permute-start | bytes 3538952 | tf_op jit(solution)/shard_map/ppermute | solution.py:438
  25.8 38.2 %collective-permute-start.1 = (bf16[18,64,512]{2,1,0:T(8,128)(2,1)}, bf16[18,64,512]{2,1,0:T(8,128)(2,1)S(1)}, u32[]{:S(2)}, u32[]{:S(2)}) collective-permute-start(bf16[18,64,512]{2,1,0:T(8,128)(2,1)} %get-tuple-element.43), channel_id=1, source_target_pairs={{128,120},{8,0},{16,8},{24,16},{32,24},{40,32},{48,40},{56,48},{64... | collective-permute-start | bytes 3538952 | tf_op jit(solution)/shard_map/ppermute | solution.py:438
  37.4 2.5 %copy-start.2 = (bf16[18,64,512]{2,1,0:T(8,128)(2,1)}, bf16[18,64,512]{2,1,0:T(8,128)(2,1)S(1)}, u32[]{:S(2)}) copy-start(bf16[18,64,512]{2,1,0:T(8,128)(2,1)S(1)} %collective-permute-done.3.below_ref) | copy-start | bytes 3538948
  39.9 32.3 %collective-permute-start.5 = (bf16[18,64,512]{2,1,0:T(8,128)(2,1)}, bf16[18,64,512]{2,1,0:T(8,128)(2,1)}, u32[]{:S(2)}, u32[]{:S(2)}) collective-permute-start(bf16[18,64,512]{2,1,0:T(8,128)(2,1)} %broadcast_select_fusion), channel_id=1, source_target_pairs={{0,128},{1,129},{2,130},{3,131},{252,124},{253,125},{254,126},{255... | collective-permute-start | bytes 3538952 | tf_op jit(solution)/shard_map/ppermute | solution.py:455
  62.6 1.4 copy-start
  64.0 1.0 copy-start.1
  65.0 7.2 %copy-start.3 = (bf16[18,64,512]{2,1,0:T(8,128)(2,1)}, bf16[18,64,512]{2,1,0:T(8,128)(2,1)S(1)}, u32[]{:S(2)}) copy-start(bf16[18,64,512]{2,1,0:T(8,128)(2,1)S(1)} %broadcast_select_fusion.1.token_ref) | copy-start | bytes 3538948
  65.0 34.6 %collective-permute-start.2 = (bf16[18,64,512]{2,1,0:T(8,128)(2,1)S(1)}, bf16[18,64,512]{2,1,0:T(8,128)(2,1)}, u32[]{:S(2)}, u32[]{:S(2)}) collective-permute-start(bf16[18,64,512]{2,1,0:T(8,128)(2,1)S(1)} %broadcast_select_fusion.1.token_ref), channel_id=1, source_target_pairs={{0,128},{1,129},{2,130},{3,131},{252,124},{253,125},{254,126},{255... | collective-permute-start | bytes 3538952 | tf_op jit(solution)/shard_map/ppermute | solution.py:455
  84.2 6.7 %collective-permute-start.6 = (f32[256,512]{1,0:T(8,128)}, f32[256,512]{1,0:T(8,128)S(1)}, u32[]{:S(2)}, u32[]{:S(2)}) collective-permute-start(f32[256,512]{1,0:T(8,128)} %get-tuple-element.48), channel_id=1, source_target_pairs={{0,1},{1,0},{2,3},{3,2},{4,5},{5,4},{6,7},{7,6},{8,9},{9,8},{10,11... | collective-permute-start | bytes 1572872 | tf_op jit(solution)/shard_map/ppermute | solution.py:457
  89.1 2.5 %collective-permute-start.7 = (f32[256,512]{1,0:T(8,128)}, f32[256,512]{1,0:T(8,128)S(1)}, u32[]{:S(2)}, u32[]{:S(2)}) collective-permute-start(f32[256,512]{1,0:T(8,128)} %get-tuple-element.49), channel_id=1, source_target_pairs={{0,1},{1,0},{2,3},{3,2},{4,5},{5,4},{6,7},{7,6},{8,9},{9,8},{10,11... | collective-permute-start | bytes 1572872 | tf_op jit(solution)/shard_map/ppermute | solution.py:457
  90.9 0.8 copy-start.6
  91.6 0.8 copy-start.7
  94.9 26.0 %collective-permute-start.10 = (s16[144,512]{1,0:T(8,128)(2,1)}, s16[144,512]{1,0:T(8,128)(2,1)S(1)}, u32[]{:S(2)}, u32[]{:S(2)}) collective-permute-start(s16[144,512]{1,0:T(8,128)(2,1)} %get-tuple-element.54), channel_id=1, source_target_pairs={{0,2},{1,3},{2,0},{3,1},{4,6},{5,7},{6,4},{7,5},{8,10},{9,11},{10,... | collective-permute-start | bytes 442376 | tf_op jit(solution)/shard_map/ppermute | solution.py:463
  95.7 25.2 %collective-permute-start.11 = (s16[144,512]{1,0:T(8,128)(2,1)}, s16[144,512]{1,0:T(8,128)(2,1)S(1)}, u32[]{:S(2)}, u32[]{:S(2)}) collective-permute-start(s16[144,512]{1,0:T(8,128)(2,1)} %get-tuple-element.55), channel_id=1, source_target_pairs={{0,4},{1,5},{2,6},{3,7},{4,0},{5,1},{6,2},{7,3},{8,12},{9,13},{10,... | collective-permute-start | bytes 442376 | tf_op jit(solution)/shard_map/ppermute | solution.py:463
  95.7 25.2 %collective-permute-start.12 = (s16[144,512]{1,0:T(8,128)(2,1)}, s16[144,512]{1,0:T(8,128)(2,1)S(1)}, u32[]{:S(2)}, u32[]{:S(2)}) collective-permute-start(s16[144,512]{1,0:T(8,128)(2,1)} %get-tuple-element.56), channel_id=1, source_target_pairs={{0,6},{1,7},{2,4},{3,5},{4,2},{5,3},{6,0},{7,1},{8,14},{9,15},{10,... | collective-permute-start | bytes 442376 | tf_op jit(solution)/shard_map/ppermute | solution.py:463
  111.6 13.9 %collective-permute-start.8 = (f32[256,512]{1,0:T(8,128)}, f32[256,512]{1,0:T(8,128)S(1)}, u32[]{:S(2)}, u32[]{:S(2)}) collective-permute-start(f32[256,512]{1,0:T(8,128)} %get-tuple-element.52), channel_id=1, source_target_pairs={{0,1},{1,0},{2,3},{3,2},{4,5},{5,4},{6,7},{7,6},{8,9},{9,8},{10,11... | collective-permute-start | bytes 1572872 | tf_op jit(solution)/shard_map/ppermute | solution.py:457
  120.8 4.7 %collective-permute-start.9 = (f32[256,512]{1,0:T(8,128)}, f32[256,512]{1,0:T(8,128)S(1)}, u32[]{:S(2)}, u32[]{:S(2)}) collective-permute-start(f32[256,512]{1,0:T(8,128)} %get-tuple-element.53), channel_id=1, source_target_pairs={{0,1},{1,0},{2,3},{3,2},{4,5},{5,4},{6,7},{7,6},{8,9},{9,8},{10,11... | collective-permute-start | bytes 1572872 | tf_op jit(solution)/shard_map/ppermute | solution.py:457
  120.9 0.7 copy-start.8
  120.9 0.7 copy-start.9
  120.9 0.7 copy-start.10
  125.5 0.8 copy-start.4
  126.4 0.8 copy-start.5
  129.6 5.2 %collective-permute-start.13 = (s16[144,512]{1,0:T(8,128)(2,1)}, s16[144,512]{1,0:T(8,128)(2,1)S(1)}, u32[]{:S(2)}, u32[]{:S(2)}) collective-permute-start(s16[144,512]{1,0:T(8,128)(2,1)} %get-tuple-element.58), channel_id=1, source_target_pairs={{0,2},{1,3},{2,0},{3,1},{4,6},{5,7},{6,4},{7,5},{8,10},{9,11},{10,... | collective-permute-start | bytes 442376 | tf_op jit(solution)/shard_map/ppermute | solution.py:463
  129.6 6.2 %collective-permute-start.14 = (s16[144,512]{1,0:T(8,128)(2,1)}, s16[144,512]{1,0:T(8,128)(2,1)S(1)}, u32[]{:S(2)}, u32[]{:S(2)}) collective-permute-start(s16[144,512]{1,0:T(8,128)(2,1)} %get-tuple-element.59), channel_id=1, source_target_pairs={{0,4},{1,5},{2,6},{3,7},{4,0},{5,1},{6,2},{7,3},{8,12},{9,13},{10,... | collective-permute-start | bytes 442376 | tf_op jit(solution)/shard_map/ppermute | solution.py:463
  129.7 16.4 %collective-permute-start.15 = (s16[144,512]{1,0:T(8,128)(2,1)}, s16[144,512]{1,0:T(8,128)(2,1)S(1)}, u32[]{:S(2)}, u32[]{:S(2)}) collective-permute-start(s16[144,512]{1,0:T(8,128)(2,1)} %get-tuple-element.60), channel_id=1, source_target_pairs={{0,6},{1,7},{2,4},{3,5},{4,2},{5,3},{6,0},{7,1},{8,14},{9,15},{10,... | collective-permute-start | bytes 442376 | tf_op jit(solution)/shard_map/ppermute | solution.py:463
  134.9 11.1 %copy-start.11 = (s16[144,512]{1,0:T(8,128)(2,1)}, s16[144,512]{1,0:T(8,128)(2,1)S(1)}, u32[]{:S(2)}) copy-start(s16[144,512]{1,0:T(8,128)(2,1)S(1)} %collective-permute-done.13.refs_1_) | copy-start | bytes 442372
  135.8 10.2 %copy-start.12 = (s16[144,512]{1,0:T(8,128)(2,1)}, s16[144,512]{1,0:T(8,128)(2,1)S(1)}, u32[]{:S(2)}) copy-start(s16[144,512]{1,0:T(8,128)(2,1)S(1)} %collective-permute-done.14.refs_2_) | copy-start | bytes 442372
  146.0 0.7 copy-start.13
